TPU v7x, 512 devices: a whole 4x4x16 slice. The times are simulated.
512 devices in a mesh: sy: 8 (over z_hi, y), sz: 16 (over z_lo, core), filt: 4 (over x).
Axes of the slice: x: 4, y: 4, z: 16 (z_hi: 2, z_lo: 8; z = z_hi * 8 + z_lo), core: 2. Of those that a mesh axis runs over, the one named last changes fastest.
Arguments:
- volume: bfloat16 [64, 16, 64, 128], P('filt', 'sy', 'sz'), may hold values from -6 to 6
- first_filters: bfloat16 [64, 1728], P('filt'), may hold values from -0.15625 to 0.15625
- second_filters: bfloat16 [64, 1728], P('filt'), may hold values from -0.15625 to 0.15625
- cotangent: bfloat16 [64, 16, 64, 128], P('filt', 'sy', 'sz'), may hold values from -6 to 6
Outputs:
- result: bfloat16 [64, 16, 64, 128], P('filt', 'sy', 'sz')
- grad_input: bfloat16 [64, 16, 64, 128], P('filt', 'sy', 'sz')
- first_grad: float32 [64, 1728], P('filt')
- second_grad: float32 [64, 1728], P('filt')
All inputs are finite; a program needn't handle non-finite values.
Results may differ from a plain program's by a relative error of at most 0.0075.
Values may be sent and summed in bfloat16 or wider, within the bound.
No kernel may reach another device: no remote copies, remote signals or barrier semaphores. Data moves between devices by JAX's collectives and lax.ppermute only.
A program may use at most 64 MiB of HBM per device.

v0:
```python
import jax
import jax.numpy as jnp
from jax import lax
from jax.sharding import PartitionSpec as P


def padded_2(cells, sides, width):
    for axis, dim in sides:
        count = lax.axis_size(axis)
        head = lax.slice_in_dim(cells, 0, width, axis=dim)
        tail = lax.slice_in_dim(cells, cells.shape[dim] - width, cells.shape[dim], axis=dim)
        cells = jnp.concatenate(
            [
                lax.ppermute(tail, axis, [(i, (i + 1) % count) for i in range(count)]),
                cells,
                lax.ppermute(head, axis, [((i + 1) % count, i) for i in range(count)]),
            ],
            axis=dim,
        )
    return cells


def stack_weights(filters, channels):
    row_count = filters.shape[0]
    return jnp.transpose(filters.reshape(row_count, 3, 3, 3, channels), (1, 2, 3, 0, 4))


def apply_taps(padded, stacked, flipped):
    channels, wide_y, wide_z, length = padded.shape
    span_y = wide_y - 2
    span_z = wide_z - 2
    row_count = stacked.shape[3]
    running = jnp.zeros((3 * row_count, span_y * span_z * length), jnp.float32)
    for step_y in range(3):
        for step_z in range(3):
            first_y = 2 - step_y if flipped else step_y
            first_z = 2 - step_z if flipped else step_z
            planes = padded[:, first_y : first_y + span_y, first_z : first_z + span_z, :].reshape(
                channels, -1
            )
            block = stacked[step_y, step_z].reshape(3 * row_count, channels)
            running = running + jnp.dot(block, planes, preferred_element_type=jnp.float32)
    pieces = running.reshape(3, row_count, span_y, span_z, length)
    summed = jnp.zeros((row_count, span_y, span_z, length), jnp.float32)
    for step_x in range(3):
        offset = step_x - 1 if flipped else 1 - step_x
        summed = summed + jnp.roll(pieces[step_x], offset, axis=3)
    return summed


def filter_terms(padded, delta, factor):
    channels = padded.shape[0]
    row_count, span_y, span_z, length = delta.shape
    rolled = jnp.stack([jnp.roll(delta, step_x - 1, axis=3) for step_x in range(3)]).reshape(
        3 * row_count, -1
    )
    blocks = []
    for step_y in range(3):
        for step_z in range(3):
            planes = padded[:, step_y : step_y + span_y, step_z : step_z + span_z, :].reshape(
                channels, -1
            )
            blocks.append(
                lax.dot_general(
                    rolled, planes, (((1,), (1,)), ((), ())), preferred_element_type=jnp.float32
                )
            )
    joined = jnp.stack(blocks).reshape(27, row_count, channels)
    return jnp.transpose(joined, (1, 0, 2)).reshape(row_count, 27 * channels) * factor


def with_rims(local):
    whole = lax.all_gather(local, "filt", axis=0, tiled=True)
    return padded_2(whole, (("sy", 1), ("sz", 2)), 1)


def through(delta, filters):
    row_count = filters.shape[0]
    channels = filters.shape[1] // 27
    padded = padded_2(delta, (("sy", 1), ("sz", 2)), 1)
    reshaped = filters.reshape(row_count, 3, 3, 3, channels)
    stacked = jnp.transpose(reshaped, (1, 2, 3, 4, 0))
    summed = lax.psum_scatter(
        apply_taps(padded, stacked, True).reshape(lax.axis_size("filt") * row_count, -1),
        "filt",
        scatter_dimension=0,
        tiled=True,
    )
    return summed.reshape(delta.shape)


def body(volume, first_filters, second_filters, cotangent):
    channels = first_filters.shape[1] // 27
    voxel_total = (
        volume.shape[1]
        * lax.axis_size("sy")
        * volume.shape[2]
        * lax.axis_size("sz")
        * volume.shape[3]
    )
    factor = float(voxel_total) ** (-0.5)
    padded_in = with_rims(volume)
    first_pre = apply_taps(padded_in, stack_weights(first_filters, channels), False)
    first_act = jax.nn.softplus(first_pre).astype(jnp.bfloat16)
    padded_mid = with_rims(first_act)
    second_pre = apply_taps(padded_mid, stack_weights(second_filters, channels), False)
    result = jax.nn.softplus(second_pre).astype(jnp.bfloat16)
    second_delta = (cotangent.astype(jnp.float32) * jax.nn.sigmoid(second_pre)).astype(jnp.bfloat16)
    second_grad = filter_terms(padded_mid, second_delta, factor)
    second_grad = lax.psum(second_grad, ("sy", "sz"))
    first_back = through(second_delta, second_filters)
    first_delta = (first_back * jax.nn.sigmoid(first_pre)).astype(jnp.bfloat16)
    first_grad = filter_terms(padded_in, first_delta, factor)
    first_grad = lax.psum(first_grad, ("sy", "sz"))
    grad_input = through(first_delta, first_filters).astype(jnp.bfloat16)
    return (result, grad_input, first_grad, second_grad)


def solution(mesh):
    return jax.shard_map(
        body,
        mesh=mesh,
        in_specs=(
            P("filt", "sy", "sz", None),
            P("filt", None),
            P("filt", None),
            P("filt", "sy", "sz", None),
        ),
        out_specs=(
            P("filt", "sy", "sz", None),
            P("filt", "sy", "sz", None),
            P("filt", None),
            P("filt", None),
        ),
        check_vma=False,
    )
```

profile of v0, /device:TPU:1, one launch (start us, length us, event | category | flops | bytes accessed | tf_op | source)
XLA Modules:
  0.0 624.9 jit_solution(9225655077063492037)
XLA Ops:
  7.2 10.5 %all_gather.6 = bf16[64,2,4,128]{3,2,1,0:T(4,128)(2,1)S(1)} all-gather(bf16[16,2,4,128]{3,2,1,0:T(4,128)(2,1)} %param.4), channel_id=1, replica_groups=mesh['sy'=8,'sz'=16,'filt'=4] {'filt'}, dimensions={0}, use_global_device_ids=true | all-gather | bytes 163840 | tf_op jit(solution)/shard_map/all_gather | solution.py:73
  17.8 3.2 collective-permute-start
  21.0 16.6 %collective-permute-start.1 = (bf16[64,1,4,128]{3,2,1,0:T(4,128)(2,1)S(1)}, bf16[64,1,4,128]{3,2,1,0:T(4,128)(2,1)S(1)}, u32[]{:S(2)}, u32[]{:S(2)}) collective-permute-start(bf16[64,1,4,128]{3,2,1,0:T(4,128)(2,1)S(1)} %get-tuple-element.87), channel_id=1, source_target_pairs={{64,0},{128,64},{192,128},{256,192},{320,256},{384,320},{448,384},... | collective-permute-start | bytes 196616 | tf_op jit(solution)/shard_map/ppermute | solution.py:16
  50.8 6.4 %collective-permute-start.2 = (bf16[64,4,1,128]{3,2,1,0:T(2,128)(2,1)S(1)}, bf16[64,4,1,128]{3,2,1,0:T(2,128)(2,1)S(1)}, u32[]{:S(2)}, u32[]{:S(2)}) collective-permute-start(bf16[64,4,1,128]{3,2,1,0:T(2,128)(2,1)S(1)} %get-tuple-element.36), channel_id=1, source_target_pairs={{0,4},{4,8},{8,12},{12,16},{16,20},{20,24},{24,28},{28,32},{32,36}... | collective-permute-start | bytes 196616 | tf_op jit(solution)/shard_map/ppermute | solution.py:14
  57.1 2.9 collective-permute-start.3
  60.4 3.1 collective-permute-done.3
  67.3 9.1 %all_gather.7 = bf16[64,2,4,128]{3,2,1,0:T(4,128)(2,1)S(1)} all-gather(bf16[16,2,4,128]{3,2,1,0:T(4,128)(2,1)S(1)} %get-tuple-element.8), channel_id=1, replica_groups=mesh['sy'=8,'sz'=16,'filt'=4] {'filt'}, dimensions={0}, use_global_device_ids=true | all-gather | bytes 163840 | tf_op jit(solution)/shard_map/all_gather | solution.py:73
  79.2 14.2 %collective-permute-start.5 = (bf16[64,1,4,128]{3,2,1,0:T(4,128)(2,1)S(1)}, bf16[64,1,4,128]{3,2,1,0:T(4,128)(2,1)S(1)}, u32[]{:S(2)}, u32[]{:S(2)}) collective-permute-start(bf16[64,1,4,128]{3,2,1,0:T(4,128)(2,1)S(1)} %get-tuple-element.82), channel_id=1, source_target_pairs={{64,0},{128,64},{192,128},{256,192},{320,256},{384,320},{448,384},... | collective-permute-start | bytes 196616 | tf_op jit(solution)/shard_map/ppermute | solution.py:16
  97.0 5.2 collective-permute-start.6
  102.2 9.6 %collective-permute-start.7 = (bf16[64,4,1,128]{3,2,1,0:T(2,128)(2,1)S(1)}, bf16[64,4,1,128]{3,2,1,0:T(2,128)(2,1)}, u32[]{:S(2)}, u32[]{:S(2)}) collective-permute-start(bf16[64,4,1,128]{3,2,1,0:T(2,128)(2,1)S(1)} %get-tuple-element.31), channel_id=1, source_target_pairs={{4,0},{8,4},{12,8},{16,12},{20,16},{24,20},{28,24},{32,28},{36,32}... | collective-permute-start | bytes 196616 | tf_op jit(solution)/shard_map/ppermute | solution.py:16
  113.0 2.5 pad_maximum_fusion.7
  122.3 1.9 collective-permute-start.8
  124.2 15.0 %collective-permute-start.9 = (bf16[16,1,4,128]{3,2,1,0:T(4,128)(2,1)}, bf16[16,1,4,128]{3,2,1,0:T(4,128)(2,1)S(1)}, u32[]{:S(2)}, u32[]{:S(2)}) collective-permute-start(bf16[16,1,4,128]{3,2,1,0:T(4,128)(2,1)} %get-tuple-element.124), channel_id=1, source_target_pairs={{64,0},{128,64},{192,128},{256,192},{320,256},{384,320},{448,384},... | collective-permute-start | bytes 49160 | tf_op jit(solution)/shard_map/ppermute | solution.py:16
  140.3 12.5 %collective-permute-start.10 = (bf16[16,4,1,128]{3,2,1,0:T(2,128)(2,1)S(1)}, bf16[16,4,1,128]{3,2,1,0:T(2,128)(2,1)S(1)}, u32[]{:S(2)}, u32[]{:S(2)}) collective-permute-start(bf16[16,4,1,128]{3,2,1,0:T(2,128)(2,1)S(1)} %get-tuple-element.107), channel_id=1, source_target_pairs={{4,0},{8,4},{12,8},{16,12},{20,16},{24,20},{28,24},{32,28},{36,32}... | collective-permute-start | bytes 49160 | tf_op jit(solution)/shard_map/ppermute | solution.py:16
  153.7 2.1 collective-permute-start.11
  156.0 8.1 %collective-permute-done.11 = bf16[16,4,1,128]{3,2,1,0:T(2,128)(2,1)S(1)} collective-permute-done((bf16[16,4,1,128]{3,2,1,0:T(2,128)(2,1)S(1)}, bf16[16,4,1,128]{3,2,1,0:T(2,128)(2,1)S(1)}, u32[]{:S(2)}, u32[]{:S(2)}) %collective-permute-start.11) | collective-permute-done | bytes 16416 | tf_op jit(solution)/shard_map/ppermute | solution.py:14
  176.1 32.3 %reduce-scatter.3.cloned.1.call-done = f32[16,1024]{1,0:T(8,128)} async-done(((f32[64,1024]{1,0:T(8,128)}), f32[16,1024]{1,0:T(8,128)}) %reduce-scatter.3.cloned.1.call-update) | async-done | bytes 65552 | tf_op jit(solution)/shard_map/reduce_scatter | solution.py:83
  212.6 3.1 collective-permute-start.12
  215.7 13.5 %collective-permute-start.13 = (bf16[16,1,4,128]{3,2,1,0:T(4,128)(2,1)S(1)}, bf16[16,1,4,128]{3,2,1,0:T(4,128)(2,1)S(1)}, u32[]{:S(2)}, u32[]{:S(2)}) collective-permute-start(bf16[16,1,4,128]{3,2,1,0:T(4,128)(2,1)S(1)} %get-tuple-element.122), channel_id=1, source_target_pairs={{64,0},{128,64},{192,128},{256,192},{320,256},{384,320},{448,384},... | collective-permute-start | bytes 49160 | tf_op jit(solution)/shard_map/ppermute | solution.py:16
  230.2 5.6 collective-permute-start.14
  236.0 2.8 collective-permute-start.15
  239.1 4.1 collective-permute-done.15
  253.5 31.4 %reduce-scatter.5.cloned.1.call-done = f32[16,1024]{1,0:T(8,128)} async-done(((f32[64,1024]{1,0:T(8,128)}), f32[16,1024]{1,0:T(8,128)}) %reduce-scatter.5.cloned.1.call-update) | async-done | bytes 65552 | tf_op jit(solution)/shard_map/reduce_scatter | solution.py:83
  286.4 329.8 %all-reduce.3.cloned.1.call-done = (f32[16,1728]{1,0:T(8,128)}, f32[16,1728]{1,0:T(8,128)}) async-done(((f32[16,1728]{1,0:T(8,128)}, f32[16,1728]{1,0:T(8,128)}), (f32[16,1728]{1,0:T(8,128)}, f32[16,1728]{1,0:T(8,128)})) %all-reduce.3.cloned.1.call-update) | async-done | bytes 221200 | tf_op jit(solution)/shard_map/psum | solution.py:114
  (318 shorter events, 63.9 us)
Async XLA Ops:
  7.2 201.3 %reduce-scatter.3.cloned.1.call-start = ((), (), s32[]{:S(2)}) async-start(), calls=%async_computation.2 | async-start | bytes 327680 | tf_op jit(solution)/shard_map/reduce_scatter | solution.py:83
  17.7 19.9 %copy-start.21 = (bf16[16,1728]{1,0:T(8,128)(2,1)S(1)}, bf16[16,1728]{1,0:T(8,128)(2,1)}, u32[]{:S(2)}) copy-start(bf16[16,1728]{1,0:T(8,128)(2,1)} %param.5) | copy-start | bytes 165892
  17.8 32.5 %collective-permute-start = (bf16[64,1,4,128]{3,2,1,0:T(4,128)(2,1)S(1)}, bf16[64,1,4,128]{3,2,1,0:T(4,128)(2,1)S(1)}, u32[]{:S(2)}, u32[]{:S(2)}) collective-permute-start(bf16[64,1,4,128]{3,2,1,0:T(4,128)(2,1)S(1)} %get-tuple-element.88), channel_id=1, source_target_pairs={{0,64},{64,128},{128,192},{192,256},{256,320},{320,384},{384,448},... | collective-permute-start | bytes 196616 | tf_op jit(solution)/shard_map/ppermute | solution.py:14
  21.0 29.3 %collective-permute-start.1 = (bf16[64,1,4,128]{3,2,1,0:T(4,128)(2,1)S(1)}, bf16[64,1,4,128]{3,2,1,0:T(4,128)(2,1)S(1)}, u32[]{:S(2)}, u32[]{:S(2)}) collective-permute-start(bf16[64,1,4,128]{3,2,1,0:T(4,128)(2,1)S(1)} %get-tuple-element.87), channel_id=1, source_target_pairs={{64,0},{128,64},{192,128},{256,192},{320,256},{384,320},{448,384},... | collective-permute-start | bytes 196616 | tf_op jit(solution)/shard_map/ppermute | solution.py:16
  50.8 9.6 %collective-permute-start.2 = (bf16[64,4,1,128]{3,2,1,0:T(2,128)(2,1)S(1)}, bf16[64,4,1,128]{3,2,1,0:T(2,128)(2,1)S(1)}, u32[]{:S(2)}, u32[]{:S(2)}) collective-permute-start(bf16[64,4,1,128]{3,2,1,0:T(2,128)(2,1)S(1)} %get-tuple-element.36), channel_id=1, source_target_pairs={{0,4},{4,8},{8,12},{12,16},{16,20},{20,24},{24,28},{28,32},{32,36}... | collective-permute-start | bytes 196616 | tf_op jit(solution)/shard_map/ppermute | solution.py:14
  57.1 6.3 %collective-permute-start.3 = (bf16[64,4,1,128]{3,2,1,0:T(2,128)(2,1)S(1)}, bf16[64,4,1,128]{3,2,1,0:T(2,128)(2,1)S(1)}, u32[]{:S(2)}, u32[]{:S(2)}) collective-permute-start(bf16[64,4,1,128]{3,2,1,0:T(2,128)(2,1)S(1)} %get-tuple-element.35), channel_id=1, source_target_pairs={{4,0},{8,4},{12,8},{16,12},{20,16},{24,20},{28,24},{32,28},{36,32}... | collective-permute-start | bytes 196616 | tf_op jit(solution)/shard_map/ppermute | solution.py:16
  67.3 27.9 %copy-start.1 = (f32[16,2,4,128]{3,2,1,0:T(4,128)}, f32[16,2,4,128]{3,2,1,0:T(4,128)S(1)}, u32[]{:S(2)}) copy-start(f32[16,2,4,128]{3,2,1,0:T(4,128)S(1)} %get-tuple-element.9) | copy-start | bytes 196612
  67.3 28.6 %copy-start.3 = (f32[16,2,4,128]{3,2,1,0:T(4,128)}, f32[16,2,4,128]{3,2,1,0:T(4,128)S(1)}, u32[]{:S(2)}) copy-start(f32[16,2,4,128]{3,2,1,0:T(4,128)S(1)} %get-tuple-element.10) | copy-start | bytes 196612
  77.3 19.2 %collective-permute-start.4 = (bf16[64,1,4,128]{3,2,1,0:T(4,128)(2,1)S(1)}, bf16[64,1,4,128]{3,2,1,0:T(4,128)(2,1)S(1)}, u32[]{:S(2)}, u32[]{:S(2)}) collective-permute-start(bf16[64,1,4,128]{3,2,1,0:T(4,128)(2,1)S(1)} %get-tuple-element.83), channel_id=1, source_target_pairs={{0,64},{64,128},{128,192},{192,256},{256,320},{320,384},{384,448},... | collective-permute-start | bytes 196616 | tf_op jit(solution)/shard_map/ppermute | solution.py:14
  79.2 17.3 %collective-permute-start.5 = (bf16[64,1,4,128]{3,2,1,0:T(4,128)(2,1)S(1)}, bf16[64,1,4,128]{3,2,1,0:T(4,128)(2,1)S(1)}, u32[]{:S(2)}, u32[]{:S(2)}) collective-permute-start(bf16[64,1,4,128]{3,2,1,0:T(4,128)(2,1)S(1)} %get-tuple-element.82), channel_id=1, source_target_pairs={{64,0},{128,64},{192,128},{256,192},{320,256},{384,320},{448,384},... | collective-permute-start | bytes 196616 | tf_op jit(solution)/shard_map/ppermute | solution.py:16
  97.0 15.4 %collective-permute-start.6 = (bf16[64,4,1,128]{3,2,1,0:T(2,128)(2,1)S(1)}, bf16[64,4,1,128]{3,2,1,0:T(2,128)(2,1)}, u32[]{:S(2)}, u32[]{:S(2)}) collective-permute-start(bf16[64,4,1,128]{3,2,1,0:T(2,128)(2,1)S(1)} %get-tuple-element.30), channel_id=1, source_target_pairs={{0,4},{4,8},{8,12},{12,16},{16,20},{20,24},{24,28},{28,32},{32,36}... | collective-permute-start | bytes 196616 | tf_op jit(solution)/shard_map/ppermute | solution.py:14
  102.2 10.8 %collective-permute-start.7 = (bf16[64,4,1,128]{3,2,1,0:T(2,128)(2,1)S(1)}, bf16[64,4,1,128]{3,2,1,0:T(2,128)(2,1)}, u32[]{:S(2)}, u32[]{:S(2)}) collective-permute-start(bf16[64,4,1,128]{3,2,1,0:T(2,128)(2,1)S(1)} %get-tuple-element.31), channel_id=1, source_target_pairs={{4,0},{8,4},{12,8},{16,12},{20,16},{24,20},{28,24},{32,28},{36,32}... | collective-permute-start | bytes 196616 | tf_op jit(solution)/shard_map/ppermute | solution.py:16
  122.3 17.4 %collective-permute-start.8 = (bf16[16,1,4,128]{3,2,1,0:T(4,128)(2,1)}, bf16[16,1,4,128]{3,2,1,0:T(4,128)(2,1)S(1)}, u32[]{:S(2)}, u32[]{:S(2)}) collective-permute-start(bf16[16,1,4,128]{3,2,1,0:T(4,128)(2,1)} %get-tuple-element.123), channel_id=1, source_target_pairs={{0,64},{64,128},{128,192},{192,256},{256,320},{320,384},{384,448},... | collective-permute-start | bytes 49160 | tf_op jit(solution)/shard_map/ppermute | solution.py:14
  124.2 16.0 %collective-permute-start.9 = (bf16[16,1,4,128]{3,2,1,0:T(4,128)(2,1)}, bf16[16,1,4,128]{3,2,1,0:T(4,128)(2,1)S(1)}, u32[]{:S(2)}, u32[]{:S(2)}) collective-permute-start(bf16[16,1,4,128]{3,2,1,0:T(4,128)(2,1)} %get-tuple-element.124), channel_id=1, source_target_pairs={{64,0},{128,64},{192,128},{256,192},{320,256},{384,320},{448,384},... | collective-permute-start | bytes 49160 | tf_op jit(solution)/shard_map/ppermute | solution.py:16
  140.3 15.5 %collective-permute-start.10 = (bf16[16,4,1,128]{3,2,1,0:T(2,128)(2,1)S(1)}, bf16[16,4,1,128]{3,2,1,0:T(2,128)(2,1)S(1)}, u32[]{:S(2)}, u32[]{:S(2)}) collective-permute-start(bf16[16,4,1,128]{3,2,1,0:T(2,128)(2,1)S(1)} %get-tuple-element.107), channel_id=1, source_target_pairs={{4,0},{8,4},{12,8},{16,12},{20,16},{24,20},{28,24},{32,28},{36,32}... | collective-permute-start | bytes 49160 | tf_op jit(solution)/shard_map/ppermute | solution.py:16
  153.7 10.4 %collective-permute-start.11 = (bf16[16,4,1,128]{3,2,1,0:T(2,128)(2,1)S(1)}, bf16[16,4,1,128]{3,2,1,0:T(2,128)(2,1)S(1)}, u32[]{:S(2)}, u32[]{:S(2)}) collective-permute-start(bf16[16,4,1,128]{3,2,1,0:T(2,128)(2,1)S(1)} %get-tuple-element.108), channel_id=1, source_target_pairs={{0,4},{4,8},{8,12},{12,16},{16,20},{20,24},{24,28},{28,32},{32,36}... | collective-permute-start | bytes 49160 | tf_op jit(solution)/shard_map/ppermute | solution.py:14
  174.0 110.9 %reduce-scatter.5.cloned.1.call-start = ((), (), s32[]{:S(2)}) async-start(), calls=%async_computation.3 | async-start | bytes 327680 | tf_op jit(solution)/shard_map/reduce_scatter | solution.py:83
  176.1 33.2 %copy-start.2 = (f32[16,2,4,128]{3,2,1,0:T(4,128)S(1)}, f32[16,2,4,128]{3,2,1,0:T(4,128)}, u32[]{:S(2)}) copy-start(f32[16,2,4,128]{3,2,1,0:T(4,128)} %copy-done.1) | copy-start | bytes 196612
  176.1 33.2 %copy-start.4 = (f32[16,2,4,128]{3,2,1,0:T(4,128)S(1)}, f32[16,2,4,128]{3,2,1,0:T(4,128)}, u32[]{:S(2)}) copy-start(f32[16,2,4,128]{3,2,1,0:T(4,128)} %copy-done.3) | copy-start | bytes 196612
  212.6 17.1 %collective-permute-start.12 = (bf16[16,1,4,128]{3,2,1,0:T(4,128)(2,1)S(1)}, bf16[16,1,4,128]{3,2,1,0:T(4,128)(2,1)S(1)}, u32[]{:S(2)}, u32[]{:S(2)}) collective-permute-start(bf16[16,1,4,128]{3,2,1,0:T(4,128)(2,1)S(1)} %get-tuple-element.121), channel_id=1, source_target_pairs={{0,64},{64,128},{128,192},{192,256},{256,320},{320,384},{384,448},... | collective-permute-start | bytes 49160 | tf_op jit(solution)/shard_map/ppermute | solution.py:14
  215.7 14.4 %collective-permute-start.13 = (bf16[16,1,4,128]{3,2,1,0:T(4,128)(2,1)S(1)}, bf16[16,1,4,128]{3,2,1,0:T(4,128)(2,1)S(1)}, u32[]{:S(2)}, u32[]{:S(2)}) collective-permute-start(bf16[16,1,4,128]{3,2,1,0:T(4,128)(2,1)S(1)} %get-tuple-element.122), channel_id=1, source_target_pairs={{64,0},{128,64},{192,128},{256,192},{320,256},{384,320},{448,384},... | collective-permute-start | bytes 49160 | tf_op jit(solution)/shard_map/ppermute | solution.py:16
  230.2 8.7 %collective-permute-start.14 = (bf16[16,4,1,128]{3,2,1,0:T(2,128)(2,1)S(1)}, bf16[16,4,1,128]{3,2,1,0:T(2,128)(2,1)S(1)}, u32[]{:S(2)}, u32[]{:S(2)}) collective-permute-start(bf16[16,4,1,128]{3,2,1,0:T(2,128)(2,1)S(1)} %get-tuple-element.105), channel_id=1, source_target_pairs={{4,0},{8,4},{12,8},{16,12},{20,16},{24,20},{28,24},{32,28},{36,32}... | collective-permute-start | bytes 49160 | tf_op jit(solution)/shard_map/ppermute | solution.py:16
  236.0 7.2 %collective-permute-start.15 = (bf16[16,4,1,128]{3,2,1,0:T(2,128)(2,1)S(1)}, bf16[16,4,1,128]{3,2,1,0:T(2,128)(2,1)S(1)}, u32[]{:S(2)}, u32[]{:S(2)}) collective-permute-start(bf16[16,4,1,128]{3,2,1,0:T(2,128)(2,1)S(1)} %get-tuple-element.106), channel_id=1, source_target_pairs={{0,4},{4,8},{8,12},{12,16},{16,20},{20,24},{24,28},{28,32},{32,36}... | collective-permute-start | bytes 49160 | tf_op jit(solution)/shard_map/ppermute | solution.py:14
  250.7 365.4 %all-reduce.3.cloned.1.call-start = ((), (), s32[]{:S(2)}) async-start(), calls=%async_computation.4 | async-start | bytes 458752 | tf_op jit(solution)/shard_map/psum | solution.py:114
  (34 other events, 109.9 us)
Sparse Core Ops, SparseCore 0:
  174.1 34.2 reduce-scatter.2
  250.9 33.9 reduce-scatter.4
  289.0 327.1 all-reduce.2
where the time goes:
time: 627 us; the launch traced here: 625 us
  waiting for transfers between devices  410 us (65%)
  starting transfers between devices  117 us (19%)
  local copies, waits for them, and re-layouts  41.1 us (7%)
  blocking collectives  19.6 us (3%)
  between operations  15.5 us (2%)
  matrix products  11.7 us (2%)
  other arithmetic  10 us (2%)
    psum x1, waiting for transfers between devices, body(): first_grad = lax.psum(first_grad, ('sy', 'sz'))  330 us
    ppermute x8, starting transfers between devices, padded_2(): lax.ppermute(head, axis, [((i + 1) % count, i) for i in range(count)])  89.9 us
    reduce_scatter x2, waiting for transfers between devices, through(): lax.psum_scatter(apply_taps(padded, stacked, True).reshape(lax.axis_size(...  63.6 us
    ppermute x8, starting transfers between devices, padded_2(): lax.ppermute(tail, axis, [(i, (i + 1) % count) for i in range(count)])  26.7 us
    all_gather x2, blocking collectives, with_rims(): whole = lax.all_gather(local, 'filt', axis=0, tiled=True)  19.6 us
    unnamed x82, local copies, waits for them, and re-layouts  13.6 us
  transfers between devices with their start and end apart: 19, of which 9 were waited for; matrix products, arithmetic and copies ran while one was open for 3% of the time, Pallas kernels for 0%

commit v1 on v0

v1 whole, which is shorter than its diff:
```python
import jax
import jax.numpy as jnp
from jax import lax
from jax.experimental import pallas as pl
from jax.experimental.pallas import tpu as pltpu
from jax.sharding import PartitionSpec as P

BF = jnp.bfloat16
F32 = jnp.float32
C = 64
Y = 16
SY = 8
SZ = 16
FILT = 4
ZB = 4
XB = 4
RIM = 4
XW = XB + 2 * RIM
HALF = 2048
GRADS = 2 * HALF
PIECE = GRADS // 8
COLUMNS = 27 * C
PARAMS = pltpu.CompilerParams(vmem_limit_bytes=48 * 1024 * 1024)


def lanes_of(shape):
    return lax.broadcasted_iota(jnp.int32, shape, len(shape) - 1)


def turned(x, shift):
    return pltpu.roll(x, shift % x.shape[-1], x.ndim - 1)


def call(kernel, out_shape, scratch, *args):
    return pl.pallas_call(
        kernel, out_shape=out_shape, scratch_shapes=scratch, compiler_params=PARAMS
    )(*args)


def pack_kernel(volume_ref, cotangent_ref, out_ref, held):
    held[0:128, :] = volume_ref[...].astype(F32)
    held[128:256, :] = cotangent_ref[...].astype(F32)
    rows = [held[pl.ds(yz, 32, stride=8), :] for yz in range(8)]
    slot = lanes_of((32, 128)) // 16
    for k in range(SY * FILT):
        total = turned(rows[0], RIM - XB * k)
        for yz in range(1, 8):
            total = jnp.where(slot == yz, turned(rows[yz], 16 * yz + RIM - XB * k), total)
        out_ref[k] = total.astype(BF)


def unpack_kernel(in_ref, out_ref, held):
    for sy in range(SY):
        block = jnp.concatenate(
            [in_ref[sy * FILT + f, 16 * vc : 16 * vc + 16, :] for vc in range(2) for f in range(FILT)],
            axis=0,
        )
        flipped = jnp.transpose(block.astype(F32))
        for yy in range(2):
            for z in range(ZB):
                first = (yy * ZB + z) * 16
                held[pl.ds(z * XW * Y + 2 * sy + yy, XW, stride=Y), :] = flipped[first : first + XW, :]
    out_ref[...] = held[...].astype(BF)


def y_taps(x):
    cells = x.shape[0] // Y
    split = x.reshape(cells, Y, 128)
    before = pltpu.roll(split, 1, 1).reshape(x.shape)
    after = pltpu.roll(split, Y - 1, 1).reshape(x.shape)
    return before, after


def store_taps(ref, z, x):
    before, after = y_taps(x)
    low = lanes_of(x.shape) < C
    ref[z, :, 0:128] = jnp.where(low, before, x).astype(BF)
    ref[z, :, 128:256] = after.astype(BF)


def softplus(x):
    return jnp.maximum(x, 0.0) + jnp.log1p(jnp.exp(-jnp.abs(x)))


def sigmoid(x):
    e = jnp.exp(-jnp.abs(x))
    return jnp.where(x >= 0, 1.0, e) / (1.0 + e)


def tap_column(a, b, c):
    return (9 * a + 3 * b + c) * C


def fill_forward(ref, filters_ref):
    ref[...] = jnp.zeros_like(ref)
    for b in range(3):
        for a in range(3):
            for at, c in ((0, 0), (1, 1), (2, 2), (3, 2)):
                first = tap_column(a, b, c)
                ref[at * C : at * C + C, b * 256 + a * C : b * 256 + a * C + C] = filters_ref[
                    :, first : first + C
                ]


def fill_backward(ref, filters_ref):
    ref[...] = jnp.zeros_like(ref)
    for b in range(3):
        for a in range(3):
            for at, c in ((0, 0), (1, 1), (2, 2), (3, 2)):
                first = tap_column(2 - a, 2 - b, 2 - c)
                ref[b * 256 + a * C : b * 256 + a * C + C, at * C : at * C + C] = filters_ref[
                    :, first : first + C
                ]


def convolved(taps_ref, weights, z, wide, transposed):
    rows = wide * Y
    planes = jnp.concatenate([taps_ref[z + b, 0:rows, :] for b in range(3)], axis=1)
    dims = (((1,), (1 if transposed else 0,)), ((), ()))
    sums = lax.dot_general(planes, weights, dims, preferred_element_type=F32)
    left, right = sums[:, 0:128], sums[:, 128:256]
    swapped = turned(left, C)
    kept = rows - 2 * Y
    low = lanes_of((kept, 128)) < C
    return (
        jnp.where(
            low,
            left[0:kept] + swapped[Y : Y + kept],
            left[Y : Y + kept] + swapped[0:kept],
        )
        + right[2 * Y : 2 * Y + kept]
    )


def main_kernel(
    below_ref, own_ref, above_ref, first_ref, second_ref, out_ref,
    field, act, delta_2, delta_1, pre_1, cells_0, cells_1, cells_2, cells_3, weights, weights_t,
):
    slabs = (below_ref, own_ref, above_ref)
    plane = XW * Y

    def slab_rows(z, first, count):
        start = (z % ZB) * plane + first
        return slabs[z // ZB][start : start + count, :].astype(F32)

    fill_forward(weights.at[0], first_ref)
    fill_forward(weights.at[1], second_ref)
    fill_backward(weights_t.at[0], first_ref)
    fill_backward(weights_t.at[1], second_ref)
    for z in range(12):
        x = slab_rows(z, 0, plane)
        before, after = y_taps(x)
        low = lanes_of(x.shape) < C
        field[z, :, 0:128] = jnp.where(low, before, turned(x, C)).astype(BF)
        field[z, :, 128:256] = after.astype(BF)
    for z in range(10):
        pre = convolved(field, weights[0], z, 12, True)
        pre_1[z] = pre
        store_taps(act, z, softplus(pre).astype(BF).astype(F32))
    for z in range(8):
        pre = convolved(act, weights[1], z, 10, True)
        cotangent = slab_rows(z + 2, 2 * Y, 8 * Y)
        low = lanes_of(cotangent.shape) < C
        cotangent = jnp.where(low, turned(cotangent, C), cotangent)
        delta = (cotangent * sigmoid(pre)).astype(BF).astype(F32)
        store_taps(delta_2, z, delta)
        if 2 <= z < 6:
            own = slice((z - 2) * 64, (z - 1) * 64)
            cells_0[own, :] = softplus(pre[2 * Y : 6 * Y])
            cells_2[own, :] = delta[2 * Y : 6 * Y]
    for z in range(6):
        back = convolved(delta_2, weights_t[1], z, 8, False)
        delta = (back * sigmoid(pre_1[z + 2, 2 * Y : 8 * Y, :])).astype(BF).astype(F32)
        store_taps(delta_1, z, delta)
        if 1 <= z < 5:
            cells_3[(z - 1) * 64 : z * 64, :] = delta[Y : 5 * Y]
    for z in range(4):
        cells_1[z * 64 : z * 64 + 64, :] = convolved(delta_1, weights_t[0], z, 6, False)

    row = lax.broadcasted_iota(jnp.int32, (256, 256), 0)
    col = lax.broadcasted_iota(jnp.int32, (256, 256), 1)
    order = (row // 64) * 64 + (row % Y) * XB + (row // Y) % XB
    reorder = jnp.where(order == col, 1.0, 0.0).astype(BF)
    for at, cells in enumerate((cells_0, cells_1)):
        flat = jnp.transpose(cells[...])[0:C, :].astype(BF)
        out_ref[:, GRADS + at * 256 : GRADS + at * 256 + 256] = jnp.dot(
            flat, reorder, preferred_element_type=F32
        ).astype(BF)
    for base, cells, source, at in ((0, cells_3, field, 3), (HALF, cells_2, act, 2)):
        flat = jnp.transpose(cells[...])[0:C, :].astype(BF)
        for b in range(3):
            for c in range(3):
                near = jnp.concatenate(
                    [source[at + b + z, (at + c) * Y : (at + c + 4) * Y, :] for z in range(4)], axis=0
                )
                sums = jnp.dot(flat, near, preferred_element_type=F32).astype(BF)
                for a in range(3):
                    first = base + tap_column(a, b, c)
                    out_ref[:, first : first + C] = sums[:, a * C : a * C + C]
        out_ref[:, base + COLUMNS : base + HALF] = jnp.zeros((C, HALF - COLUMNS), BF)


def split_kernel(in_ref, out_ref):
    for q in range(8):
        total = in_ref[0, :, q * PIECE : (q + 1) * PIECE].astype(F32)
        for f in range(1, FILT):
            total = total + in_ref[f, :, q * PIECE : (q + 1) * PIECE].astype(F32)
        out_ref[q * 16 : q * 16 + 16, 0:PIECE] = total.astype(BF)
    for q in range(8):
        for f in range(FILT):
            out_ref[q * 16 : q * 16 + 16, PIECE + f * C : PIECE + f * C + C] = in_ref[
                f, :, GRADS + q * C : GRADS + q * C + C
            ]


def relay_kernel(in_ref, out_ref):
    total = jnp.sum(in_ref[:, 0:PIECE].astype(F32), axis=0, keepdims=True)
    out_ref[:, 0:PIECE] = jnp.broadcast_to(total, (128, PIECE)).astype(BF)
    row = lax.broadcasted_iota(jnp.int32, (256, 256), 0)
    col = lax.broadcasted_iota(jnp.int32, (256, 256), 1)
    order = ((row // 8) % SY) * 32 + (row // 64) * 8 + row % 8
    reorder = jnp.where(order == col, 1.0, 0.0).astype(BF)
    cells = jnp.dot(in_ref[:, PIECE : PIECE + 256], reorder, preferred_element_type=F32)
    slot = lanes_of((16, 128)) // 32
    for to in range(SY):
        for tile in range(2):
            total = None
            for at in range(4):
                sy = tile * 4 + at
                piece = cells[sy * 16 : sy * 16 + 16, (to // 4) * 128 : (to // 4) * 128 + 128]
                piece = turned(piece, (at - to % 4) * 32) if at != to % 4 else piece
                total = piece if total is None else jnp.where(slot == at, piece, total)
            first = PIECE + tile * 128
            out_ref[to * 16 : to * 16 + 16, first : first + 128] = total.astype(BF)


def finish_kernel(factor, in_ref, result_ref, grad_input_ref, first_ref, second_ref, held):
    for base, ref in ((0, first_ref), (4, second_ref)):
        for q in range(4):
            wide = min(PIECE, COLUMNS - q * PIECE)
            start = (base + q) * 16
            ref[:, q * PIECE : q * PIECE + wide] = in_ref[start : start + 16, 0:wide].astype(F32) * factor
    row = lax.broadcasted_iota(jnp.int32, (256, 256), 0)
    col = lax.broadcasted_iota(jnp.int32, (256, 256), 1)
    order = ((row // 4) % 2) * 128 + (row // 8) * 4 + row % 4
    reorder = jnp.where(order == col, 1.0, 0.0).astype(BF)
    cells = jnp.dot(in_ref[:, PIECE : PIECE + 256], reorder, preferred_element_type=F32)
    for at, ref in enumerate((result_ref, grad_input_ref)):
        for z in range(ZB):
            for yy in range(2):
                start = (at * ZB + z) * 16
                held[at, pl.ds(yy * ZB + z, 16, stride=8), :] = cells[
                    start : start + 16, yy * 128 : yy * 128 + 128
                ]
        ref[...] = held[at].astype(BF)


def body(volume, first_filters, second_filters, cotangent):
    shape = jax.ShapeDtypeStruct
    factor = float(SY * volume.shape[1] * SZ * volume.shape[2] * volume.shape[3]) ** -0.5
    with jax.named_scope("pack_windows"):
        packed = call(
            pack_kernel, shape((SY * FILT, 32, 128), BF), [pltpu.VMEM((256, 128), F32)],
            volume.reshape(128, 128), cotangent.reshape(128, 128),
        )
    with jax.named_scope("windows_exchange"):
        windows = lax.all_to_all(packed, ("sy", "filt"), 0, 0, tiled=True)
    with jax.named_scope("unpack_windows"):
        own = call(
            unpack_kernel, shape((ZB * XW * Y, 128), BF), [pltpu.VMEM((ZB * XW * Y, 128), F32)], windows
        )
    with jax.named_scope("z_rim_exchange"):
        below = lax.ppermute(own, "sz", [(i, (i + 1) % SZ) for i in range(SZ)])
        above = lax.ppermute(own, "sz", [((i + 1) % SZ, i) for i in range(SZ)])
    with jax.named_scope("filters_gather"):
        filters = lax.all_gather(jnp.concatenate([first_filters, second_filters], axis=1), "filt", axis=0, tiled=True)
        first, second = filters[:, :COLUMNS], filters[:, COLUMNS:]
    with jax.named_scope("layers"):
        partial = call(
            main_kernel,
            shape((C, GRADS + 512), BF),
            [
                pltpu.VMEM((12, 12 * Y, 256), BF),
                pltpu.VMEM((10, 10 * Y, 256), BF),
                pltpu.VMEM((8, 8 * Y, 256), BF),
                pltpu.VMEM((6, 6 * Y, 256), BF),
                pltpu.VMEM((10, 10 * Y, 128), F32),
                pltpu.VMEM((256, 128), F32),
                pltpu.VMEM((256, 128), F32),
                pltpu.VMEM((256, 128), F32),
                pltpu.VMEM((256, 128), F32),
                pltpu.VMEM((2, 256, 768), BF),
                pltpu.VMEM((2, 768, 256), BF),
            ],
            below, own, above, first, second,
        )
    with jax.named_scope("channel_exchange"):
        shares = lax.all_to_all(partial.reshape(FILT, 16, GRADS + 512), "filt", 0, 0, tiled=True)
    with jax.named_scope("split_shares"):
        rows = call(split_kernel, shape((128, PIECE + 256), BF), [], shares)
    with jax.named_scope("sum_exchange"):
        rows = lax.all_to_all(rows, ("sy", "sz"), 0, 0, tiled=True)
    with jax.named_scope("sum_and_relay"):
        rows = call(relay_kernel, shape((128, PIECE + 256), BF), [], rows)
    with jax.named_scope("spread_exchange"):
        rows = lax.all_to_all(rows, ("sy", "sz"), 0, 0, tiled=True)
    with jax.named_scope("finish"):
        result, grad_input, first_grad, second_grad = call(
            lambda *refs: finish_kernel(factor, *refs),
            (
                shape((128, 128), BF), shape((128, 128), BF),
                shape((16, COLUMNS), F32), shape((16, COLUMNS), F32),
            ),
            [pltpu.VMEM((2, 128, 128), F32)],
            rows,
        )
    return (result.reshape(volume.shape), grad_input.reshape(volume.shape), first_grad, second_grad)


def solution(mesh):
    return jax.shard_map(
        body,
        mesh=mesh,
        in_specs=(
            P("filt", "sy", "sz", None),
            P("filt", None),
            P("filt", None),
            P("filt", "sy", "sz", None),
        ),
        out_specs=(
            P("filt", "sy", "sz", None),
            P("filt", "sy", "sz", None),
            P("filt", None),
            P("filt", None),
        ),
        check_vma=False,
    )
```

time: 627 us -> 137 us (0.22)
  waiting for transfers between devices: 410 us -> 10.2 us
  starting transfers between devices: 117 us -> 35.8 us
  blocking collectives: 19.6 us -> 78.8 us
  local copies, waits for them, and re-layouts: 41.1 us -> 2.61 us
  between operations: 15.5 us -> 0.75 us
  matrix products: 11.7 us -> 0 us
  other arithmetic: 10 us -> 1.54 us
  Pallas kernels: 0 us -> 6.94 us
    psum x1 -> x0, waiting for transfers between devices: 330 us -> none  [body(): first_grad = lax.psum(first_grad, ('sy', 'sz'))]
    ppermute x16 -> x2, starting transfers between devices: 117 us -> 14.5 us  [the longest x1 12.6 us: body(): below = lax.ppermute(own, 'sz', [(i, (i + 1) % SZ) for i in range(SZ)])]
    all_to_all x0 -> x3, blocking collectives: none -> 67.1 us  [the longest x2 55.6 us: body(): rows = lax.all_to_all(rows, ('sy', 'sz'), 0, 0, tiled=True)]
    reduce_scatter x2 -> x0, waiting for transfers between devices: 63.6 us -> none  [through(): lax.psum_scatter(apply_taps(padded, stacked, True).reshape(lax.axis_size(...]
    all_to_all x0 -> x1, starting transfers between devices: none -> 21.3 us  [body(): windows = lax.all_to_all(packed, ('sy', 'filt'), 0, 0, tiled=True)]
    ppermute x16 -> x2, waiting for transfers between devices: 16.8 us -> 4.92 us  [the longest x1 4.18 us: body(): above = lax.ppermute(own, 'sz', [((i + 1) % SZ, i) for i in range(SZ)])]
    unnamed x82 -> x14, local copies, waits for them, and re-layouts: 13.6 us -> 1.96 us
    dot_general x54 -> x0, matrix products: 11.7 us -> none  [the longest x36 9 us: apply_taps(): jnp.dot(block, planes, preferred_element_type=jnp.float32)]
  transfers between devices with their start and end apart: 19 -> 3, of which waited for: 9 -> 3; matrix products, arithmetic and copies ran while one was open for 3% -> 0% of each run, Pallas kernels for 0% -> 0%
where the time goes in v1:
time: 137 us
  blocking collectives  78.8 us (58%)
  starting transfers between devices  35.8 us (26%)
  waiting for transfers between devices  10.2 us (7%)
  Pallas kernels  6.94 us (5%)
  local copies, waits for them, and re-layouts  2.61 us (2%)
  other arithmetic  1.54 us (1%)
    all_to_all x2, blocking collectives, body(): rows = lax.all_to_all(rows, ('sy', 'sz'), 0, 0, tiled=True)  55.6 us
    all_to_all x1, starting transfers between devices, body(): windows = lax.all_to_all(packed, ('sy', 'filt'), 0, 0, tiled=True)  21.3 us
    ppermute x1, starting transfers between devices, body(): below = lax.ppermute(own, 'sz', [(i, (i + 1) % SZ) for i in range(SZ)])  12.6 us
    all_gather x1, blocking collectives, body(): lax.all_gather(jnp.concatenate([first_filters, second_filters], axis=1),...  11.7 us
    all_to_all x1, blocking collectives, body(): lax.all_to_all(partial.reshape(FILT, 16, GRADS + 512), 'filt', 0, 0, tile...  11.5 us
    pallas_call x6, Pallas kernels, call(): pl.pallas_call(kernel, out_shape=out_shape, scratch_shapes=scratch, compi...  6.94 us
    all_to_all x1, waiting for transfers between devices, body(): windows = lax.all_to_all(packed, ('sy', 'filt'), 0, 0, tiled=True)  5.26 us
    ppermute x1, waiting for transfers between devices, body(): above = lax.ppermute(own, 'sz', [((i + 1) % SZ, i) for i in range(SZ)])  4.18 us
  transfers between devices with their start and end apart: 3, of which 3 were waited for; matrix products, arithmetic and copies ran while one was open for 0% of the time, Pallas kernels for 0%

profile of v1, /device:TPU:1, one launch (start us, length us, event | category | flops | bytes accessed | tf_op | source)
XLA Modules:
  0.0 136.6 jit_solution(16688768891105025798)
XLA Ops:
  0.6 0.7 copy-done
  1.4 0.8 copy-done.1
  2.1 1.3 pack_windows.1
  3.5 21.3 %all-to-all-start = ((bf16[32,32,128]{2,1,0:T(8,128)(2,1)}), bf16[32,32,128]{2,1,0:T(8,128)(2,1)S(1)}, u32[]{:S(2)}, u32[]{:S(2)}) async-start(bf16[32,32,128]{2,1,0:T(8,128)(2,1)} %pack_windows.1), calls=%async_computation | async-start | bytes 524288 | tf_op jit(solution)/shard_map/windows_exchange/all_to_all | solution.py:267
  24.8 11.7 %all_gather.3 = bf16[64,3456]{1,0:T(8,128)(2,1)S(1)} all-gather(bf16[16,3456]{1,0:T(8,128)(2,1)S(1)} %pad_maximum_fusion), channel_id=1, replica_groups=mesh['sy'=8,'sz'=16,'filt'=4] {'filt'}, dimensions={0}, use_global_device_ids=true | all-gather | bytes 552960 | tf_op jit(solution)/shard_map/filters_gather/all_gather | solution.py:276
  36.5 5.3 %all-to-all-done.in_ref = bf16[32,32,128]{2,1,0:T(8,128)(2,1)S(1)} async-done(((bf16[32,32,128]{2,1,0:T(8,128)(2,1)}), bf16[32,32,128]{2,1,0:T(8,128)(2,1)S(1)}, u32[]{:S(2)}, u32[]{:S(2)}) %all-to-all-start) | async-done | bytes 262176 | tf_op jit(solution)/shard_map/windows_exchange/all_to_all | solution.py:267
  41.8 0.2 unpack_windows.1.own_ref
  42.0 12.6 %collective-permute-start = (bf16[768,128]{1,0:T(8,128)(2,1)S(1)}, bf16[768,128]{1,0:T(8,128)(2,1)S(1)}, u32[]{:S(2)}, u32[]{:S(2)}) collective-permute-start(bf16[768,128]{1,0:T(8,128)(2,1)S(1)} %unpack_windows.1.own_ref), channel_id=1, source_target_pairs={{0,4},{4,8},{8,12},{12,16},{16,20},{20,24},{24,28},{28,32},{32,36}... | collective-permute-start | bytes 589832 | tf_op jit(solution)/shard_map/z_rim_exchange/ppermute | solution.py:273
  54.6 1.9 %collective-permute-start.1 = (bf16[768,128]{1,0:T(8,128)(2,1)S(1)}, bf16[768,128]{1,0:T(8,128)(2,1)S(1)}, u32[]{:S(2)}, u32[]{:S(2)}) collective-permute-start(bf16[768,128]{1,0:T(8,128)(2,1)S(1)} %unpack_windows.1.own_ref), channel_id=1, source_target_pairs={{4,0},{8,4},{12,8},{16,12},{20,16},{24,20},{28,24},{32,28},{36,32}... | collective-permute-start | bytes 589832 | tf_op jit(solution)/shard_map/z_rim_exchange/ppermute | solution.py:274
  56.5 0.1 fusion
  56.7 0.7 collective-permute-done.below_ref
  57.4 4.2 %collective-permute-done.1.above_ref = bf16[768,128]{1,0:T(8,128)(2,1)S(1)} collective-permute-done((bf16[768,128]{1,0:T(8,128)(2,1)S(1)}, bf16[768,128]{1,0:T(8,128)(2,1)S(1)}, u32[]{:S(2)}, u32[]{:S(2)}) %collective-permute-start.1) | collective-permute-done | bytes 196640 | tf_op jit(solution)/shard_map/z_rim_exchange/ppermute | solution.py:274
  61.6 4.2 %layers.1 = bf16[64,4608]{1,0:T(8,128)(2,1)S(1)} custom-call(bf16[768,128]{1,0:T(8,128)(2,1)S(1)} %collective-permute-done.below_ref, bf16[768,128]{1,0:T(8,128)(2,1)S(1)} %unpack_windows.1.own_ref, bf16[768,128]{1,0:T(8,128)(2,1)S(1)} %collective-permute-done.1.above_ref, bf16[64,1728]{1,0:T(8,128)(2,1)S(1)} %get-tuple-element.13.first_ref, ...), custom_call_target="tpu_custom_call" | custom-call | tf_op jit(solution)/shard_map/layers/pallas_call | solution.py:35
  65.8 11.5 %all_to_all.32.in_ref = bf16[4,16,4608]{2,1,0:T(8,128)(2,1)S(1)} all-to-all(bf16[4,16,4608]{2,1,0:T(8,128)(2,1)S(1)} %bitcast.13), channel_id=1, replica_groups=mesh['sy'=8,'sz'=16,'filt'=4] {'filt'}, dimensions={0} | all-to-all | bytes 1179648 | tf_op jit(solution)/shard_map/channel_exchange/all_to_all | solution.py:298
  77.3 0.1 split_shares.1
  77.4 0.5 broadcast
  77.9 0.7 reduce
  78.7 29.0 %all_to_all.33 = bf16[128,2,384]{2,1,0:T(2,128)(2,1)S(1)} all-to-all(bf16[128,2,384]{2,1,0:T(2,128)(2,1)S(1)} %reshape.32), channel_id=1, replica_groups=mesh['sy'=8,'sz'=16,'filt'=4] {'sy','sz'}, dimensions={0} | all-to-all | bytes 393216 | tf_op jit(solution)/shard_map/sum_exchange/all_to_all | solution.py:302
  107.7 0.1 reshape.33
  107.9 0.3 sum_and_relay.1
  108.2 0.7 reduce.1
  109.0 26.6 %all_to_all.34 = bf16[128,2,384]{2,1,0:T(2,128)(2,1)S(1)} all-to-all(bf16[128,2,384]{2,1,0:T(2,128)(2,1)S(1)} %reshape.34), channel_id=1, replica_groups=mesh['sy'=8,'sz'=16,'filt'=4] {'sy','sz'}, dimensions={0} | all-to-all | bytes 393216 | tf_op jit(solution)/shard_map/spread_exchange/all_to_all | solution.py:306
  135.6 0.1 reshape.35
  135.8 0.9 finish.1
  (11 shorter events, 0.3 us)
Async XLA Ops:
  0.6 0.8 copy-start
  1.4 0.8 copy-start.1
  3.5 21.3 %copy-start.2 = (bf16[16,1728]{1,0:T(8,128)(2,1)S(1)}, bf16[16,1728]{1,0:T(8,128)(2,1)}, u32[]{:S(2)}) copy-start(bf16[16,1728]{1,0:T(8,128)(2,1)} %param.6) | copy-start | bytes 165892
  3.5 21.3 %copy-start.3 = (bf16[16,1728]{1,0:T(8,128)(2,1)S(1)}, bf16[16,1728]{1,0:T(8,128)(2,1)}, u32[]{:S(2)}) copy-start(bf16[16,1728]{1,0:T(8,128)(2,1)} %param.5) | copy-start | bytes 165892
  3.5 38.3 %all-to-all-start = ((bf16[32,32,128]{2,1,0:T(8,128)(2,1)}), bf16[32,32,128]{2,1,0:T(8,128)(2,1)S(1)}, u32[]{:S(2)}, u32[]{:S(2)}) async-start(bf16[32,32,128]{2,1,0:T(8,128)(2,1)} %pack_windows.1), calls=%async_computation | async-start | bytes 524288 | tf_op jit(solution)/shard_map/windows_exchange/all_to_all | solution.py:267
  42.0 15.4 %collective-permute-start = (bf16[768,128]{1,0:T(8,128)(2,1)S(1)}, bf16[768,128]{1,0:T(8,128)(2,1)S(1)}, u32[]{:S(2)}, u32[]{:S(2)}) collective-permute-start(bf16[768,128]{1,0:T(8,128)(2,1)S(1)} %unpack_windows.1.own_ref), channel_id=1, source_target_pairs={{0,4},{4,8},{8,12},{12,16},{16,20},{20,24},{24,28},{28,32},{32,36}... | collective-permute-start | bytes 589832 | tf_op jit(solution)/shard_map/z_rim_exchange/ppermute | solution.py:273
  54.6 7.0 %collective-permute-start.1 = (bf16[768,128]{1,0:T(8,128)(2,1)S(1)}, bf16[768,128]{1,0:T(8,128)(2,1)S(1)}, u32[]{:S(2)}, u32[]{:S(2)}) collective-permute-start(bf16[768,128]{1,0:T(8,128)(2,1)S(1)} %unpack_windows.1.own_ref), channel_id=1, source_target_pairs={{4,0},{8,4},{12,8},{16,12},{20,16},{24,20},{28,24},{32,28},{36,32}... | collective-permute-start | bytes 589832 | tf_op jit(solution)/shard_map/z_rim_exchange/ppermute | solution.py:274

commit v2 on v1

v2 whole, which is shorter than its diff:
```python
import jax
import jax.numpy as jnp
from jax import lax
from jax.experimental import pallas as pl
from jax.experimental.pallas import tpu as pltpu
from jax.sharding import PartitionSpec as P

BF = jnp.bfloat16
F32 = jnp.float32
C = 64
Y = 16
SY = 8
SZ = 16
FILT = 4
SYH = SY // 2
ZB = 4
XB = 8
RIM = 4
XW = XB + 2 * RIM
PLANE = XW * Y
BLOCKS = SYH * FILT
HALF = 2048
GRADS = 2 * HALF
QUARTER = GRADS // SYH
PIECE = QUARTER // 4
COLUMNS = 27 * C
PARAMS = pltpu.CompilerParams(vmem_limit_bytes=48 * 1024 * 1024)


def at_device(half, y, z, core):
    return (half * SYH + y) * SZ + z * 2 + core


PENCIL = ("sy", "sz")
HALVES, PAIRS, CORES = range(2), range(SZ // 4), range(2)
SAME_HALF = [[half * BLOCKS + i for i in range(BLOCKS)] for half in HALVES]
FOURS = [
    [at_device(half, y, 2 * pair + odd, core) for odd in HALVES for core in CORES]
    for half in HALVES for y in range(SYH) for pair in PAIRS
]
EIGHTS = [
    [at_device(half, y, 2 * pair + odd, core) for half in HALVES for pair in PAIRS]
    for y in range(SYH) for odd in HALVES for core in CORES
]
SIXTEENS = [
    [at_device(half, y, 2 * pair + odd, core) for y in range(SYH) for odd in HALVES for core in CORES]
    for half in HALVES for pair in PAIRS
]


def along_z(step):
    pairs = []
    for half in HALVES:
        for y in range(SYH):
            for z in range(SZ):
                to = (half * SZ + z + step) % (2 * SZ)
                pairs.append((half * SYH * SZ + y * SZ + z, (to // SZ) * SYH * SZ + y * SZ + to % SZ))
    return pairs


def lanes_of(shape):
    return lax.broadcasted_iota(jnp.int32, shape, len(shape) - 1)


def turned(x, shift):
    return pltpu.roll(x, shift % x.shape[-1], x.ndim - 1)


def call(kernel, out_shape, scratch, *args):
    return pl.pallas_call(
        kernel, out_shape=out_shape, scratch_shapes=scratch, compiler_params=PARAMS
    )(*args)


def pack_kernel(volume_ref, cotangent_ref, first_ref, second_ref, out_ref, filters_ref, held):
    held[0:128, :] = volume_ref[...].astype(F32)
    held[128:256, :] = cotangent_ref[...].astype(F32)
    rows = [held[pl.ds(yz, 32, stride=8), :] for yz in range(8)]
    slot = lanes_of((32, 128)) // 16
    for k in range(BLOCKS):
        total = turned(rows[0], RIM - XB * k)
        for yz in range(1, 8):
            total = jnp.where(slot == yz, turned(rows[yz], 16 * yz + RIM - XB * k), total)
        total = total.astype(BF)
        out_ref[k] = total
        out_ref[BLOCKS + k] = total
    for f in range(FILT):
        filters_ref[f, 0] = first_ref[...]
        filters_ref[f, 1] = second_ref[...]


def unpack_kernel(in_ref, out_ref, held):
    for sy in range(SY):
        block = jnp.concatenate(
            [in_ref[sy * FILT + f, 16 * vc : 16 * vc + 16, :] for vc in range(2) for f in range(FILT)],
            axis=0,
        )
        flipped = jnp.transpose(block.astype(F32))
        for yy in range(2):
            for z in range(ZB):
                first = (yy * ZB + z) * XW
                held[pl.ds(z * PLANE + 2 * sy + yy, XW, stride=Y), :] = flipped[first : first + XW, :]
    out_ref[...] = held[...].astype(BF)


def y_taps(x):
    cells = x.shape[0] // Y
    split = x.reshape(cells, Y, 128)
    before = pltpu.roll(split, 1, 1).reshape(x.shape)
    after = pltpu.roll(split, Y - 1, 1).reshape(x.shape)
    return before, after


def store_taps(ref, z, x):
    before, after = y_taps(x)
    low = lanes_of(x.shape) < C
    ref[z, :, 0:128] = jnp.where(low, before, x).astype(BF)
    ref[z, :, 128:256] = after.astype(BF)


def softplus(x):
    return jnp.maximum(x, 0.0) + jnp.log1p(jnp.exp(-jnp.abs(x)))


def sigmoid(x):
    e = jnp.exp(-jnp.abs(x))
    return jnp.where(x >= 0, 1.0, e) / (1.0 + e)


def tap_column(a, b, c):
    return (9 * a + 3 * b + c) * C


def fill_forward(ref, filters_ref, layer):
    ref[...] = jnp.zeros_like(ref)
    for b in range(3):
        for a in range(3):
            for at, c in ((0, 0), (1, 1), (2, 2), (3, 2)):
                first = tap_column(a, b, c)
                for f in range(FILT):
                    row = at * C + f * 16
                    ref[row : row + 16, b * 256 + a * C : b * 256 + a * C + C] = filters_ref[
                        f, layer, :, first : first + C
                    ]


def fill_backward(ref, filters_ref, layer):
    ref[...] = jnp.zeros_like(ref)
    for b in range(3):
        for a in range(3):
            for at, c in ((0, 0), (1, 1), (2, 2), (3, 2)):
                first = tap_column(2 - a, 2 - b, 2 - c)
                for f in range(FILT):
                    row = b * 256 + a * C + f * 16
                    ref[row : row + 16, at * C : at * C + C] = filters_ref[
                        f, layer, :, first : first + C
                    ]


def convolved(taps_ref, weights, z, wide, transposed):
    rows = wide * Y
    planes = jnp.concatenate([taps_ref[z + b, 0:rows, :] for b in range(3)], axis=1)
    dims = (((1,), (1 if transposed else 0,)), ((), ()))
    sums = lax.dot_general(planes, weights, dims, preferred_element_type=F32)
    left, right = sums[:, 0:128], sums[:, 128:256]
    swapped = turned(left, C)
    kept = rows - 2 * Y
    low = lanes_of((kept, 128)) < C
    return (
        jnp.where(
            low,
            left[0:kept] + swapped[Y : Y + kept],
            left[Y : Y + kept] + swapped[0:kept],
        )
        + right[2 * Y : 2 * Y + kept]
    )


def main_kernel(
    below_ref, own_ref, above_ref, filters_ref, out_ref,
    field, act, delta_2, delta_1, pre_1, cells_0, cells_1, cells_2, cells_3, weights, weights_t,
):
    half = lax.axis_index("sy") // SYH
    slabs = (below_ref, own_ref, above_ref)

    def slab_rows(z, first, count):
        start = (z % ZB) * PLANE + first
        return slabs[z // ZB][start : start + count, :].astype(F32)

    for layer in range(2):
        fill_forward(weights.at[layer], filters_ref, layer)
        fill_backward(weights_t.at[layer], filters_ref, layer)
    for z in range(12):
        x = slab_rows(z, 0, PLANE)
        before, after = y_taps(x)
        low = lanes_of(x.shape) < C
        field[z, :, 0:128] = jnp.where(low, before, turned(x, C)).astype(BF)
        field[z, :, 128:256] = after.astype(BF)
    for z in range(10):
        pre = convolved(field, weights[0], z, XW, True)
        pre_1[z] = pre
        store_taps(act, z, softplus(pre).astype(BF).astype(F32))
    for z in range(8):
        pre = convolved(act, weights[1], z, XW - 2, True)
        cotangent = slab_rows(z + 2, 2 * Y, (XW - 4) * Y)
        low = lanes_of(cotangent.shape) < C
        cotangent = jnp.where(low, turned(cotangent, C), cotangent)
        delta = (cotangent * sigmoid(pre)).astype(BF).astype(F32)
        store_taps(delta_2, z, delta)
        if 2 <= z < 6:
            cells_0[z - 2] = softplus(pre[2 * Y : (2 + XB) * Y])
            cells_2[z - 2] = delta[2 * Y : (2 + XB) * Y]
    for z in range(6):
        back = convolved(delta_2, weights_t[1], z, XW - 4, False)
        delta = (back * sigmoid(pre_1[z + 2, 2 * Y : (XW - 4) * Y, :])).astype(BF).astype(F32)
        store_taps(delta_1, z, delta)
        if 1 <= z < 5:
            cells_3[z - 1] = delta[Y : (1 + XB) * Y]
    for z in range(4):
        cells_1[z] = convolved(delta_1, weights_t[0], z, XW - 6, False)

    count = ZB * XB * Y
    row = lax.broadcasted_iota(jnp.int32, (count, count // 2), 0)
    col = lax.broadcasted_iota(jnp.int32, (count, count // 2), 1)
    y = row % Y - half * (Y // 2)
    order = (y // 2) * 64 + (row // (XB * Y)) * 16 + (y % 2) * XB + (row // Y) % XB
    inside = (y >= 0) & (y < Y // 2)
    reorder = jnp.where(inside & (order == col), 1.0, 0.0).astype(BF)
    for at, cells in enumerate((cells_0, cells_1)):
        flat = jnp.transpose(cells[...].reshape(count, 128))[0:C, :].astype(BF)
        flat = jnp.dot(flat, reorder, preferred_element_type=F32).astype(BF)
        for to in range(SYH):
            first = QUARTER + at * 64
            out_ref[to, :, first : first + 64] = flat[:, to * 64 : to * 64 + 64]
    for base, cells, source, at in ((0, cells_3, field, 3), (HALF, cells_2, act, 2)):
        own = pl.ds(pl.multiple_of(half * 64, 64), 64)
        flat = jnp.transpose(cells[:, own, :].reshape(256, 128))[0:C, :].astype(BF)
        for b in range(3):
            for c in range(3):
                near = pl.ds(pl.multiple_of((at + c) * Y + half * 64, 16), 64)
                near = jnp.concatenate([source[at + b + z, near, :] for z in range(4)], axis=0)
                sums = jnp.dot(flat, near, preferred_element_type=F32).astype(BF)
                for a in range(3):
                    first = base + tap_column(a, b, c)
                    to, first = first // QUARTER, first % QUARTER
                    out_ref[to, :, first : first + C] = sums[:, a * C : a * C + C]
        out_ref[(base + COLUMNS) // QUARTER, :, (base + COLUMNS) % QUARTER : QUARTER] = jnp.zeros(
            (C, HALF - COLUMNS), BF
        )


def split_kernel(in_ref, out_ref, result_ref, grad_input_ref, held):
    for to in range(4):
        lanes = slice(to * PIECE, (to + 1) * PIECE)
        total = in_ref[0, :, lanes].astype(F32)
        for k in range(1, BLOCKS):
            total = total + in_ref[k, :, lanes].astype(F32)
        out_ref[to] = total.astype(BF)
    blocks = [in_ref[k, :, QUARTER : QUARTER + 128].astype(F32) for k in range(BLOCKS)]
    slot = lanes_of((16, 128)) // XB
    for at, ref in enumerate((result_ref, grad_input_ref)):
        for z in range(ZB):
            for yy in range(2):
                first = at * 64 + z * 16 + yy * XB
                total = turned(blocks[0], -first)
                for k in range(1, BLOCKS):
                    total = jnp.where(slot == k, turned(blocks[k], k * XB - first), total)
                held[at, pl.ds(yy * ZB + z, 16, stride=8), :] = total
        ref[...] = held[at].astype(BF)


def sum_kernel(in_ref, out_ref):
    total = in_ref[0].astype(F32)
    for k in range(1, in_ref.shape[0]):
        total = total + in_ref[k].astype(F32)
    total = total.astype(BF)
    for k in range(out_ref.shape[0]):
        out_ref[k] = total


def finish_kernel(factor, in_ref, first_ref, second_ref):
    for base, ref in ((0, first_ref), (8, second_ref)):
        for k in range(7):
            wide = min(PIECE, COLUMNS - k * PIECE)
            ref[:, k * PIECE : k * PIECE + wide] = in_ref[base + k, :, 0:wide].astype(F32) * factor


def body(volume, first_filters, second_filters, cotangent):
    shape = jax.ShapeDtypeStruct
    factor = float(SY * volume.shape[1] * SZ * volume.shape[2] * volume.shape[3]) ** -0.5
    with jax.named_scope("pack_windows"):
        packed, filters = call(
            pack_kernel,
            (shape((SY * FILT, 32, 128), BF), shape((FILT, 2, 16, COLUMNS), BF)),
            [pltpu.VMEM((256, 128), F32)],
            volume.reshape(128, 128), cotangent.reshape(128, 128), first_filters, second_filters,
        )
    with jax.named_scope("windows_exchange"):
        windows = lax.all_to_all(packed, ("sy", "filt"), 0, 0, tiled=True)
    with jax.named_scope("unpack_windows"):
        own = call(unpack_kernel, shape((ZB * PLANE, 128), BF), [pltpu.VMEM((ZB * PLANE, 128), F32)], windows)
    with jax.named_scope("z_rim_exchange"):
        below = lax.ppermute(own, PENCIL, along_z(1))
        above = lax.ppermute(own, PENCIL, along_z(-1))
    with jax.named_scope("filters_exchange"):
        filters, own = lax.optimization_barrier((filters, own))
        filters = lax.all_to_all(filters, "filt", 0, 0, tiled=True)
    with jax.named_scope("layers"):
        partial = call(
            main_kernel,
            shape((SYH, C, QUARTER + 128), BF),
            [
                pltpu.VMEM((12, XW * Y, 256), BF),
                pltpu.VMEM((10, (XW - 2) * Y, 256), BF),
                pltpu.VMEM((8, (XW - 4) * Y, 256), BF),
                pltpu.VMEM((6, (XW - 6) * Y, 256), BF),
                pltpu.VMEM((10, (XW - 2) * Y, 128), F32),
                pltpu.VMEM((ZB, XB * Y, 128), F32),
                pltpu.VMEM((ZB, XB * Y, 128), F32),
                pltpu.VMEM((ZB, XB * Y, 128), F32),
                pltpu.VMEM((ZB, XB * Y, 128), F32),
                pltpu.VMEM((2, 256, 768), BF),
                pltpu.VMEM((2, 768, 256), BF),
            ],
            below, own, above, filters,
        )
    with jax.named_scope("blocks_exchange"):
        shares = partial.reshape(BLOCKS, 16, QUARTER + 128)
        shares = lax.all_to_all(shares, ("sy", "filt"), 0, 0, tiled=True, axis_index_groups=SAME_HALF)
    with jax.named_scope("split_shares"):
        pieces, result, grad_input = call(
            split_kernel,
            (shape((4, 16, PIECE), BF), shape((128, 128), BF), shape((128, 128), BF)),
            [pltpu.VMEM((2, 128, 128), F32)],
            shares,
        )
    with jax.named_scope("near_sum_exchange"):
        pieces = lax.all_to_all(pieces, PENCIL, 0, 0, tiled=True, axis_index_groups=FOURS)
        pieces = call(sum_kernel, shape((8, 16, PIECE), BF), [], pieces)
    with jax.named_scope("far_sum_exchange"):
        pieces = lax.all_to_all(pieces, PENCIL, 0, 0, tiled=True, axis_index_groups=EIGHTS)
        pieces = call(sum_kernel, shape((16, 16, PIECE), BF), [], pieces)
    with jax.named_scope("spread_exchange"):
        pieces = lax.all_to_all(pieces, PENCIL, 0, 0, tiled=True, axis_index_groups=SIXTEENS)
    with jax.named_scope("finish"):
        first_grad, second_grad = call(
            lambda *refs: finish_kernel(factor, *refs),
            (shape((16, COLUMNS), F32), shape((16, COLUMNS), F32)),
            [],
            pieces,
        )
    return (result.reshape(volume.shape), grad_input.reshape(volume.shape), first_grad, second_grad)


def solution(mesh):
    return jax.shard_map(
        body,
        mesh=mesh,
        in_specs=(
            P("filt", "sy", "sz", None),
            P("filt", None),
            P("filt", None),
            P("filt", "sy", "sz", None),
        ),
        out_specs=(
            P("filt", "sy", "sz", None),
            P("filt", "sy", "sz", None),
            P("filt", None),
            P("filt", None),
        ),
        check_vma=False,
    )
```

time: 137 us -> 119 us (0.87)
  starting transfers between devices: 35.8 us -> 14.2 us
  blocking collectives: 78.8 us -> 88.3 us
  waiting for transfers between devices: 10.2 us -> 4.04 us
  other arithmetic: 1.54 us -> 0 us
    all_to_all x3 -> x5, blocking collectives: 67.1 us -> 88.3 us  [the longest x1 38 us: body(): windows = lax.all_to_all(packed, ('sy', 'filt'), 0, 0, tiled=True)]
    all_to_all x1, starting transfers between devices: 21.3 us -> 3.48 us  [body(): filters = lax.all_to_all(filters, 'filt', 0, 0, tiled=True)]
    all_gather x1 -> x0, blocking collectives: 11.7 us -> none  [body(): lax.all_gather(jnp.concatenate([first_filters, second_filters], axis=1),...]
    all_to_all x1, waiting for transfers between devices: 5.26 us -> 0.01 us  [body(): filters = lax.all_to_all(filters, 'filt', 0, 0, tiled=True)]
    ppermute x2, starting transfers between devices: 14.5 us -> 10.8 us  [the longest x1 8.65 us: body(): below = lax.ppermute(own, PENCIL, along_z(1))]
    all_to_all x2 -> x0, other arithmetic: 1.45 us -> none  [body(): rows = lax.all_to_all(rows, ('sy', 'sz'), 0, 0, tiled=True)]
    pallas_call x6 -> x7, Pallas kernels: 6.94 us -> 8.14 us  [call(): pl.pallas_call(kernel, out_shape=out_shape, scratch_shapes=scratch, compi...]
    unnamed x14 -> x8, local copies, waits for them, and re-layouts: 1.96 us -> 3.15 us
  transfers between devices with their start and end apart: 3 -> 3, of which waited for: 3 -> 1; matrix products, arithmetic and copies ran while one was open for 0% -> 0% of each run, Pallas kernels for 0% -> 0%
where the time goes in v2:
time: 119 us
  blocking collectives  88.3 us (74%)
  starting transfers between devices  14.2 us (12%)
  Pallas kernels  8.14 us (7%)
  waiting for transfers between devices  4.04 us (3%)
  local copies, waits for them, and re-layouts  3.15 us (3%)
    all_to_all x1, blocking collectives, body(): windows = lax.all_to_all(packed, ('sy', 'filt'), 0, 0, tiled=True)  38 us
    all_to_all x1, blocking collectives, body(): lax.all_to_all(pieces, PENCIL, 0, 0, tiled=True, axis_index_groups=EIGHTS)  16.8 us
    all_to_all x1, blocking collectives, body(): lax.all_to_all(shares, ('sy', 'filt'), 0, 0, tiled=True, axis_index_group...  14.7 us
    all_to_all x1, blocking collectives, body(): lax.all_to_all(pieces, PENCIL, 0, 0, tiled=True, axis_index_groups=SIXTEENS)  10.7 us
    ppermute x1, starting transfers between devices, body(): below = lax.ppermute(own, PENCIL, along_z(1))  8.65 us
    all_to_all x1, blocking collectives, body(): lax.all_to_all(pieces, PENCIL, 0, 0, tiled=True, axis_index_groups=FOURS)  8.22 us
    pallas_call x7, Pallas kernels, call(): pl.pallas_call(kernel, out_shape=out_shape, scratch_shapes=scratch, compi...  8.14 us
    ppermute x1, waiting for transfers between devices, body(): above = lax.ppermute(own, PENCIL, along_z(-1))  4.03 us
  transfers between devices with their start and end apart: 3, of which 1 were waited for; matrix products, arithmetic and copies ran while one was open for 0% of the time, Pallas kernels for 0%

profile of v2, /device:TPU:1, one launch (start us, length us, event | category | flops | bytes accessed | tf_op | source)
XLA Modules:
  0.0 118.5 jit_solution(11662610756830969706)
XLA Ops:
  0.6 0.0 copy-start
  0.6 0.8 copy-done
  1.5 0.0 copy-start.1
  1.5 0.8 copy-done.1
  2.3 0.0 copy-start.2
  2.3 0.8 copy-done.2
  3.0 0.0 copy-start.3
  3.0 0.8 copy-done.3
  3.8 1.1 pack_windows.1
  4.9 38.0 %all_to_all.30.in_ref = bf16[32,32,128]{2,1,0:T(8,128)(2,1)S(1)} all-to-all(bf16[32,32,128]{2,1,0:T(8,128)(2,1)S(1)} %get-tuple-element.13), channel_id=1, replica_groups=mesh['sy'=8,'sz'=16,'filt'=4] {'sy','filt'}, dimensions={0} | all-to-all | bytes 524288 | tf_op jit(solution)/shard_map/windows_exchange/all_to_all | solution.py:299
  42.8 0.2 unpack_windows.1.own_ref
  43.0 3.5 %all-to-all-start.1 = ((bf16[4,2,16,1728]{3,2,1,0:T(8,128)(2,1)}), bf16[4,2,16,1728]{3,2,1,0:T(8,128)(2,1)S(1)}, u32[]{:S(2)}, u32[]{:S(2)}) async-start(bf16[4,2,16,1728]{3,2,1,0:T(8,128)(2,1)} %get-tuple-element.16), calls=%async_computation.1 | async-start | bytes 917504 | tf_op jit(solution)/shard_map/filters_exchange/all_to_all | solution.py:307
  46.5 2.1 %collective-permute-start.1 = (bf16[1024,128]{1,0:T(8,128)(2,1)S(1)}, bf16[1024,128]{1,0:T(8,128)(2,1)S(1)}, u32[]{:S(2)}, u32[]{:S(2)}) collective-permute-start(bf16[1024,128]{1,0:T(8,128)(2,1)S(1)} %unpack_windows.1.own_ref), channel_id=1, source_target_pairs={{0,316},{4,0},{8,4},{12,8},{16,12},{20,16},{24,20},{28,24},{32,28}... | collective-permute-start | bytes 786440 | tf_op jit(solution)/shard_map/z_rim_exchange/ppermute | solution.py:304
  48.6 8.7 %collective-permute-start = (bf16[1024,128]{1,0:T(8,128)(2,1)S(1)}, bf16[1024,128]{1,0:T(8,128)(2,1)S(1)}, u32[]{:S(2)}, u32[]{:S(2)}) collective-permute-start(bf16[1024,128]{1,0:T(8,128)(2,1)S(1)} %unpack_windows.1.own_ref), channel_id=1, source_target_pairs={{0,4},{4,8},{8,12},{12,16},{16,20},{20,24},{24,28},{28,32},{32,36}... | collective-permute-start | bytes 786440 | tf_op jit(solution)/shard_map/z_rim_exchange/ppermute | solution.py:303
  57.3 4.0 %collective-permute-done.1.above_ref = bf16[1024,128]{1,0:T(8,128)(2,1)S(1)} collective-permute-done((bf16[1024,128]{1,0:T(8,128)(2,1)S(1)}, bf16[1024,128]{1,0:T(8,128)(2,1)S(1)}, u32[]{:S(2)}, u32[]{:S(2)}) %collective-permute-start.1) | collective-permute-done | bytes 262176 | tf_op jit(solution)/shard_map/z_rim_exchange/ppermute | solution.py:304
  61.3 0.0 collective-permute-done.below_ref
  61.3 0.0 all-to-all-done.1.filters_ref
  61.3 5.2 %layers.1 = bf16[4,64,1152]{2,1,0:T(8,128)(2,1)S(1)} custom-call(bf16[1024,128]{1,0:T(8,128)(2,1)S(1)} %collective-permute-done.below_ref, bf16[1024,128]{1,0:T(8,128)(2,1)S(1)} %unpack_windows.1.own_ref, bf16[1024,128]{1,0:T(8,128)(2,1)S(1)} %collective-permute-done.1.above_ref, bf16[4,2,16,1728]{3,2,1,0:T(8,128)(2,1)S(1)} %all-to-all-done.1.filters_ref), custom_call_target="tpu_custom_call" | custom-call | tf_op jit(solution)/shard_map/layers/pallas_call | solution.py:70
  66.5 14.7 %all_to_all.31.in_ref = bf16[16,16,1152]{2,1,0:T(8,128)(2,1)S(1)} all-to-all(bf16[16,16,1152]{2,1,0:T(8,128)(2,1)S(1)} %bitcast.5), channel_id=1, replica_groups={{0,1,2,3,64,65,66,67,128,129,130,131,192,193,194,195},{256,257,258,259,..., dimensions={0} | all-to-all | bytes 1179648 | tf_op jit(solution)/shard_map/blocks_exchange/all_to_all | solution.py:329
  81.2 1.0 split_shares.1
  82.1 8.2 %all_to_all.32.in_ref = bf16[4,16,256]{2,1,0:T(8,128)(2,1)S(1)} all-to-all(bf16[4,16,256]{2,1,0:T(8,128)(2,1)S(1)} %get-tuple-element.19), channel_id=1, replica_groups={{0,4,8,12},{16,20,24,28},{32,36,40,44},{48,52,56,60},{64,68,72,76},{80,..., dimensions={0} | all-to-all | bytes 65536 | tf_op jit(solution)/shard_map/near_sum_exchange/all_to_all | solution.py:338
  90.4 16.8 %all_to_all.33.in_ref = bf16[8,16,256]{2,1,0:T(8,128)(2,1)S(1)} all-to-all(bf16[8,16,256]{2,1,0:T(8,128)(2,1)S(1)} %near_sum_exchange.1), channel_id=1, replica_groups={{0,16,32,48,256,272,288,304},{4,20,36,52,260,276,292,308},{8,24,40,56,2..., dimensions={0} | all-to-all | bytes 131072 | tf_op jit(solution)/shard_map/far_sum_exchange/all_to_all | solution.py:341
  107.2 10.7 %all_to_all.34.refs_0_ = bf16[16,16,256]{2,1,0:T(8,128)(2,1)S(1)} all-to-all(bf16[16,16,256]{2,1,0:T(8,128)(2,1)S(1)} %far_sum_exchange.1), channel_id=1, replica_groups={{0,4,8,12,64,68,72,76,128,132,136,140,192,196,200,204},{16,20,24,28,80,..., dimensions={0} | all-to-all | bytes 262144 | tf_op jit(solution)/shard_map/spread_exchange/all_to_all | solution.py:344
  117.8 0.7 finish.1
  (2 shorter events, 0.0 us)
Async XLA Ops:
  0.6 0.8 copy-start
  1.5 0.8 copy-start.1
  2.3 0.8 copy-start.2
  3.0 0.8 copy-start.3
  43.0 18.3 %all-to-all-start.1 = ((bf16[4,2,16,1728]{3,2,1,0:T(8,128)(2,1)}), bf16[4,2,16,1728]{3,2,1,0:T(8,128)(2,1)S(1)}, u32[]{:S(2)}, u32[]{:S(2)}) async-start(bf16[4,2,16,1728]{3,2,1,0:T(8,128)(2,1)} %get-tuple-element.16), calls=%async_computation.1 | async-start | bytes 917504 | tf_op jit(solution)/shard_map/filters_exchange/all_to_all | solution.py:307
  46.5 14.8 %collective-permute-start.1 = (bf16[1024,128]{1,0:T(8,128)(2,1)S(1)}, bf16[1024,128]{1,0:T(8,128)(2,1)S(1)}, u32[]{:S(2)}, u32[]{:S(2)}) collective-permute-start(bf16[1024,128]{1,0:T(8,128)(2,1)S(1)} %unpack_windows.1.own_ref), channel_id=1, source_target_pairs={{0,316},{4,0},{8,4},{12,8},{16,12},{20,16},{24,20},{28,24},{32,28}... | collective-permute-start | bytes 786440 | tf_op jit(solution)/shard_map/z_rim_exchange/ppermute | solution.py:304
  48.6 12.7 %collective-permute-start = (bf16[1024,128]{1,0:T(8,128)(2,1)S(1)}, bf16[1024,128]{1,0:T(8,128)(2,1)S(1)}, u32[]{:S(2)}, u32[]{:S(2)}) collective-permute-start(bf16[1024,128]{1,0:T(8,128)(2,1)S(1)} %unpack_windows.1.own_ref), channel_id=1, source_target_pairs={{0,4},{4,8},{8,12},{12,16},{16,20},{20,24},{24,28},{28,32},{32,36}... | collective-permute-start | bytes 786440 | tf_op jit(solution)/shard_map/z_rim_exchange/ppermute | solution.py:303

commit v3 on v2

--- a/solution.py
+++ b/solution.py
@@ -19,10 +19,11 @@
 XW = XB + 2 * RIM
 PLANE = XW * Y
 BLOCKS = SYH * FILT
-HALF = 2048
+HALF = 28 * C
 GRADS = 2 * HALF
 QUARTER = GRADS // SYH
-PIECE = QUARTER // 4
+PIECE = 256
+TILES = HALF // (SYH // 2) // 128
 COLUMNS = 27 * C
 PARAMS = pltpu.CompilerParams(vmem_limit_bytes=48 * 1024 * 1024)
 
@@ -72,27 +73,37 @@
     )(*args)
 
 
-def pack_kernel(volume_ref, cotangent_ref, first_ref, second_ref, out_ref, filters_ref, held):
-    held[0:128, :] = volume_ref[...].astype(F32)
-    held[128:256, :] = cotangent_ref[...].astype(F32)
-    rows = [held[pl.ds(yz, 32, stride=8), :] for yz in range(8)]
-    slot = lanes_of((32, 128)) // 16
+def pack_kernel(near_ref, far_ref, first_ref, second_ref, out_ref, held, filters):
+    filters[...] = jnp.zeros_like(filters)
+    filters[:, 0:COLUMNS] = first_ref[...]
+    filters[:, HALF : HALF + COLUMNS] = second_ref[...]
+    share = lax.axis_index("sy") % SYH
+    for tile in range(TILES):
+        first = pl.multiple_of((share * TILES + tile) * 128, 128)
+        columns = filters[:, pl.ds(first, 128)]
+        for k in range(BLOCKS):
+            out_ref[k, 64 + 16 * tile : 80 + 16 * tile, :] = columns
+    lower = lax.axis_index("sy") < SYH
+    near, far = near_ref[...].astype(F32), far_ref[...].astype(F32)
+    held[0:256, :] = jnp.where(lower, near, far)
+    held[256:512, :] = jnp.where(lower, far, near)
+    rows = [held[pl.ds(yz, 64, stride=8), :] for yz in range(8)]
+    slot = lanes_of((64, 128)) // 16
     for k in range(BLOCKS):
         total = turned(rows[0], RIM - XB * k)
         for yz in range(1, 8):
             total = jnp.where(slot == yz, turned(rows[yz], 16 * yz + RIM - XB * k), total)
-        total = total.astype(BF)
-        out_ref[k] = total
-        out_ref[BLOCKS + k] = total
-    for f in range(FILT):
-        filters_ref[f, 0] = first_ref[...]
-        filters_ref[f, 1] = second_ref[...]
+        out_ref[k, 0:64, :] = total.astype(BF)
 
 
 def unpack_kernel(in_ref, out_ref, held):
     for sy in range(SY):
+        top = (sy // SYH) * 32
         block = jnp.concatenate(
-            [in_ref[sy * FILT + f, 16 * vc : 16 * vc + 16, :] for vc in range(2) for f in range(FILT)],
+            [
+                in_ref[(sy % SYH) * FILT + f, top + 16 * vc : top + 16 * vc + 16, :]
+                for vc in range(2) for f in range(FILT)
+            ],
             axis=0,
         )
         flipped = jnp.transpose(block.astype(F32))
@@ -131,30 +142,35 @@
     return (9 * a + 3 * b + c) * C
 
 
-def fill_forward(ref, filters_ref, layer):
+def filter_block(windows_ref, layer, f, a, b, c):
+    column = layer * HALF + tap_column(a, b, c)
+    tile = column // 128
+    top = 64 + 16 * (tile % TILES)
+    return windows_ref[(tile // TILES) * FILT + f, top : top + 16, column % 128 : column % 128 + C]
+
+
+def fill_forward(ref, windows_ref, layer):
     ref[...] = jnp.zeros_like(ref)
     for b in range(3):
         for a in range(3):
             for at, c in ((0, 0), (1, 1), (2, 2), (3, 2)):
-                first = tap_column(a, b, c)
                 for f in range(FILT):
                     row = at * C + f * 16
-                    ref[row : row + 16, b * 256 + a * C : b * 256 + a * C + C] = filters_ref[
-                        f, layer, :, first : first + C
-                    ]
-
-
-def fill_backward(ref, filters_ref, layer):
+                    ref[row : row + 16, b * 256 + a * C : b * 256 + a * C + C] = filter_block(
+                        windows_ref, layer, f, a, b, c
+                    )
+
+
+def fill_backward(ref, windows_ref, layer):
     ref[...] = jnp.zeros_like(ref)
     for b in range(3):
         for a in range(3):
             for at, c in ((0, 0), (1, 1), (2, 2), (3, 2)):
-                first = tap_column(2 - a, 2 - b, 2 - c)
                 for f in range(FILT):
                     row = b * 256 + a * C + f * 16
-                    ref[row : row + 16, at * C : at * C + C] = filters_ref[
-                        f, layer, :, first : first + C
-                    ]
+                    ref[row : row + 16, at * C : at * C + C] = filter_block(
+                        windows_ref, layer, f, 2 - a, 2 - b, 2 - c
+                    )
 
 
 def convolved(taps_ref, weights, z, wide, transposed):
@@ -177,7 +193,7 @@
 
 
 def main_kernel(
-    below_ref, own_ref, above_ref, filters_ref, out_ref,
+    below_ref, own_ref, above_ref, windows_ref, out_ref,
     field, act, delta_2, delta_1, pre_1, cells_0, cells_1, cells_2, cells_3, weights, weights_t,
 ):
     half = lax.axis_index("sy") // SYH
@@ -188,8 +204,8 @@
         return slabs[z // ZB][start : start + count, :].astype(F32)
 
     for layer in range(2):
-        fill_forward(weights.at[layer], filters_ref, layer)
-        fill_backward(weights_t.at[layer], filters_ref, layer)
+        fill_forward(weights.at[layer], windows_ref, layer)
+        fill_backward(weights_t.at[layer], windows_ref, layer)
     for z in range(12):
         x = slab_rows(z, 0, PLANE)
         before, after = y_taps(x)
@@ -249,13 +265,19 @@
         )
 
 
-def split_kernel(in_ref, out_ref, result_ref, grad_input_ref, held):
+def split_kernel(in_ref, out_ref):
     for to in range(4):
-        lanes = slice(to * PIECE, (to + 1) * PIECE)
+        wide = min(PIECE, QUARTER - to * PIECE)
+        lanes = slice(to * PIECE, to * PIECE + wide)
         total = in_ref[0, :, lanes].astype(F32)
         for k in range(1, BLOCKS):
             total = total + in_ref[k, :, lanes].astype(F32)
-        out_ref[to] = total.astype(BF)
+        out_ref[to, :, 0:wide] = total.astype(BF)
+        if wide < PIECE:
+            out_ref[to, :, wide:PIECE] = jnp.zeros((16, PIECE - wide), BF)
+
+
+def outputs_kernel(in_ref, result_ref, grad_input_ref, held):
     blocks = [in_ref[k, :, QUARTER : QUARTER + 128].astype(F32) for k in range(BLOCKS)]
     slot = lanes_of((16, 128)) // XB
     for at, ref in enumerate((result_ref, grad_input_ref)):
@@ -280,31 +302,32 @@
 
 def finish_kernel(factor, in_ref, first_ref, second_ref):
     for base, ref in ((0, first_ref), (8, second_ref)):
-        for k in range(7):
-            wide = min(PIECE, COLUMNS - k * PIECE)
-            ref[:, k * PIECE : k * PIECE + wide] = in_ref[base + k, :, 0:wide].astype(F32) * factor
+        for k in range(8):
+            first = (k // 4) * QUARTER + (k % 4) * PIECE
+            wide = min(PIECE, QUARTER - (k % 4) * PIECE, COLUMNS - first)
+            ref[:, first : first + wide] = in_ref[base + k, :, 0:wide].astype(F32) * factor
 
 
 def body(volume, first_filters, second_filters, cotangent):
     shape = jax.ShapeDtypeStruct
     factor = float(SY * volume.shape[1] * SZ * volume.shape[2] * volume.shape[3]) ** -0.5
+    with jax.named_scope("halves_exchange"):
+        near = jnp.concatenate([volume.reshape(128, 128), cotangent.reshape(128, 128)], axis=0)
+        far = lax.ppermute(near, "sy", [(i, (i + SYH) % SY) for i in range(SY)])
     with jax.named_scope("pack_windows"):
-        packed, filters = call(
+        packed = call(
             pack_kernel,
-            (shape((SY * FILT, 32, 128), BF), shape((FILT, 2, 16, COLUMNS), BF)),
-            [pltpu.VMEM((256, 128), F32)],
-            volume.reshape(128, 128), cotangent.reshape(128, 128), first_filters, second_filters,
+            shape((BLOCKS, 64 + 16 * TILES, 128), BF),
+            [pltpu.VMEM((512, 128), F32), pltpu.VMEM((16, 2 * HALF), BF)],
+            near, far, first_filters, second_filters,
         )
     with jax.named_scope("windows_exchange"):
-        windows = lax.all_to_all(packed, ("sy", "filt"), 0, 0, tiled=True)
+        windows = lax.all_to_all(packed, ("sy", "filt"), 0, 0, tiled=True, axis_index_groups=SAME_HALF)
     with jax.named_scope("unpack_windows"):
         own = call(unpack_kernel, shape((ZB * PLANE, 128), BF), [pltpu.VMEM((ZB * PLANE, 128), F32)], windows)
     with jax.named_scope("z_rim_exchange"):
         below = lax.ppermute(own, PENCIL, along_z(1))
         above = lax.ppermute(own, PENCIL, along_z(-1))
-    with jax.named_scope("filters_exchange"):
-        filters, own = lax.optimization_barrier((filters, own))
-        filters = lax.all_to_all(filters, "filt", 0, 0, tiled=True)
     with jax.named_scope("layers"):
         partial = call(
             main_kernel,
@@ -322,15 +345,17 @@
                 pltpu.VMEM((2, 256, 768), BF),
                 pltpu.VMEM((2, 768, 256), BF),
             ],
-            below, own, above, filters,
+            below, own, above, windows,
         )
     with jax.named_scope("blocks_exchange"):
         shares = partial.reshape(BLOCKS, 16, QUARTER + 128)
         shares = lax.all_to_all(shares, ("sy", "filt"), 0, 0, tiled=True, axis_index_groups=SAME_HALF)
     with jax.named_scope("split_shares"):
-        pieces, result, grad_input = call(
-            split_kernel,
-            (shape((4, 16, PIECE), BF), shape((128, 128), BF), shape((128, 128), BF)),
+        pieces = call(split_kernel, shape((4, 16, PIECE), BF), [], shares)
+    with jax.named_scope("place_outputs"):
+        result, grad_input = call(
+            outputs_kernel,
+            (shape((128, 128), BF), shape((128, 128), BF)),
             [pltpu.VMEM((2, 128, 128), F32)],
             shares,
         )

time: 119 us -> 110 us (0.924)
  blocking collectives: 88.3 us -> 62.7 us
  starting transfers between devices: 14.2 us -> 26.3 us
  waiting for transfers between devices: 4.04 us -> 11.2 us
  local copies, waits for them, and re-layouts: 3.15 us -> 0.01 us
    all_to_all x2 -> x1, blocking collectives: 48.6 us -> 16.9 us  [body(): lax.all_to_all(packed, ('sy', 'filt'), 0, 0, tiled=True, axis_index_group...]
    ppermute x0 -> x1, starting transfers between devices: none -> 16.3 us  [body(): far = lax.ppermute(near, 'sy', [(i, (i + SYH) % SY) for i in range(SY)])]
    ppermute x1, starting transfers between devices: 8.65 us -> 0.3 us  [body(): below = lax.ppermute(own, PENCIL, along_z(1))]
    all_to_all x1, waiting for transfers between devices: 0.01 us -> 5.27 us  [body(): lax.all_to_all(pieces, PENCIL, 0, 0, tiled=True, axis_index_groups=SIXTEENS)]
    all_to_all x1, blocking collectives: 16.8 us -> 21.4 us  [body(): lax.all_to_all(pieces, PENCIL, 0, 0, tiled=True, axis_index_groups=EIGHTS)]
    all_to_all x1, blocking collectives: 8.22 us -> 12.6 us  [body(): lax.all_to_all(pieces, PENCIL, 0, 0, tiled=True, axis_index_groups=FOURS)]
    unnamed x8 -> x4, local copies, waits for them, and re-layouts: 3.15 us -> 0.01 us
    all_to_all x1, blocking collectives: 14.7 us -> 11.7 us  [body(): lax.all_to_all(shares, ('sy', 'filt'), 0, 0, tiled=True, axis_index_group...]
  transfers between devices with their start and end apart: 3 -> 4, of which waited for: 1 -> 3; matrix products, arithmetic and copies ran while one was open for 0% -> 0% of each run, Pallas kernels for 0% -> 1%
where the time goes in v3:
time: 110 us
  blocking collectives  62.7 us (57%)
  starting transfers between devices  26.3 us (24%)
  waiting for transfers between devices  11.2 us (10%)
  Pallas kernels  8.5 us (8%)
    all_to_all x1, blocking collectives, body(): lax.all_to_all(pieces, PENCIL, 0, 0, tiled=True, axis_index_groups=EIGHTS)  21.4 us
    all_to_all x1, blocking collectives, body(): lax.all_to_all(packed, ('sy', 'filt'), 0, 0, tiled=True, axis_index_group...  16.9 us
    ppermute x1, starting transfers between devices, body(): far = lax.ppermute(near, 'sy', [(i, (i + SYH) % SY) for i in range(SY)])  16.3 us
    all_to_all x1, blocking collectives, body(): lax.all_to_all(pieces, PENCIL, 0, 0, tiled=True, axis_index_groups=FOURS)  12.6 us
    all_to_all x1, blocking collectives, body(): lax.all_to_all(shares, ('sy', 'filt'), 0, 0, tiled=True, axis_index_group...  11.7 us
    pallas_call x8, Pallas kernels, call(): pl.pallas_call(kernel, out_shape=out_shape, scratch_shapes=scratch, compi...  8.5 us
    all_to_all x1, starting transfers between devices, body(): lax.all_to_all(pieces, PENCIL, 0, 0, tiled=True, axis_index_groups=SIXTEENS)  5.32 us
    all_to_all x1, waiting for transfers between devices, body(): lax.all_to_all(pieces, PENCIL, 0, 0, tiled=True, axis_index_groups=SIXTEENS)  5.27 us
  transfers between devices with their start and end apart: 4, of which 3 were waited for; matrix products, arithmetic and copies ran while one was open for 0% of the time, Pallas kernels for 1%

profile of v3, /device:TPU:1, one launch (start us, length us, event | category | flops | bytes accessed | tf_op | source)
XLA Modules:
  0.0 110.1 jit_solution(12225866483973538860)
XLA Ops:
  0.6 0.0 copy-start
  0.6 0.0 copy-start.1
  0.7 0.8 pad_maximum_fusion.near_ref
  1.5 16.3 %collective-permute-start = (bf16[256,128]{1,0:T(8,128)(2,1)S(1)}, bf16[256,128]{1,0:T(8,128)(2,1)S(1)}, u32[]{:S(2)}, u32[]{:S(2)}) collective-permute-start(bf16[256,128]{1,0:T(8,128)(2,1)S(1)} %pad_maximum_fusion.near_ref), channel_id=1, source_target_pairs={{0,256},{64,320},{128,384},{192,448},{256,0},{320,64},{384,128},{4... | collective-permute-start | bytes 196616 | tf_op jit(solution)/shard_map/halves_exchange/ppermute | solution.py:316
  17.7 1.8 %collective-permute-done.far_ref = bf16[256,128]{1,0:T(8,128)(2,1)S(1)} collective-permute-done((bf16[256,128]{1,0:T(8,128)(2,1)S(1)}, bf16[256,128]{1,0:T(8,128)(2,1)S(1)}, u32[]{:S(2)}, u32[]{:S(2)}) %collective-permute-start) | collective-permute-done | bytes 65568 | tf_op jit(solution)/shard_map/halves_exchange/ppermute | solution.py:316
  19.6 0.0 copy-done
  19.6 0.0 copy-done.1
  19.6 0.7 pack_windows.1
  20.3 16.9 %all_to_all.25.in_ref.windows_ref = bf16[16,176,128]{2,1,0:T(8,128)(2,1)S(1)} all-to-all(bf16[16,176,128]{2,1,0:T(8,128)(2,1)S(1)} %pack_windows.1), channel_id=1, replica_groups={{0,1,2,3,64,65,66,67,128,129,130,131,192,193,194,195},{256,257,258,259,..., dimensions={0} | all-to-all | bytes 1441792 | tf_op jit(solution)/shard_map/windows_exchange/all_to_all | solution.py:325
  37.2 0.2 unpack_windows.1.own_ref
  37.4 4.4 %collective-permute-start.2 = (bf16[1024,128]{1,0:T(8,128)(2,1)S(1)}, bf16[1024,128]{1,0:T(8,128)(2,1)S(1)}, u32[]{:S(2)}, u32[]{:S(2)}) collective-permute-start(bf16[1024,128]{1,0:T(8,128)(2,1)S(1)} %unpack_windows.1.own_ref), channel_id=1, source_target_pairs={{0,316},{4,0},{8,4},{12,8},{16,12},{20,16},{24,20},{28,24},{32,28}... | collective-permute-start | bytes 786440 | tf_op jit(solution)/shard_map/z_rim_exchange/ppermute | solution.py:330
  41.8 0.3 collective-permute-start.1
  42.1 4.0 %collective-permute-done.2.above_ref = bf16[1024,128]{1,0:T(8,128)(2,1)S(1)} collective-permute-done((bf16[1024,128]{1,0:T(8,128)(2,1)S(1)}, bf16[1024,128]{1,0:T(8,128)(2,1)S(1)}, u32[]{:S(2)}, u32[]{:S(2)}) %collective-permute-start.2) | collective-permute-done | bytes 262176 | tf_op jit(solution)/shard_map/z_rim_exchange/ppermute | solution.py:330
  46.2 0.0 collective-permute-done.1.below_ref
  46.2 5.2 %layers.1 = bf16[4,64,1024]{2,1,0:T(8,128)(2,1)S(1)} custom-call(bf16[1024,128]{1,0:T(8,128)(2,1)S(1)} %collective-permute-done.1.below_ref, bf16[1024,128]{1,0:T(8,128)(2,1)S(1)} %unpack_windows.1.own_ref, bf16[1024,128]{1,0:T(8,128)(2,1)S(1)} %collective-permute-done.2.above_ref, bf16[16,176,128]{2,1,0:T(8,128)(2,1)S(1)} %all_to_all.25.in_ref.windows_ref), custom_call_target="tpu_custom_call" | custom-call | tf_op jit(solution)/shard_map/layers/pallas_call | solution.py:71
  51.3 11.7 %all_to_all.26.in_ref = bf16[16,16,1024]{2,1,0:T(8,128)(2,1)S(1)} all-to-all(bf16[16,16,1024]{2,1,0:T(8,128)(2,1)S(1)} %bitcast.5), channel_id=1, replica_groups={{0,1,2,3,64,65,66,67,128,129,130,131,192,193,194,195},{256,257,258,259,..., dimensions={0} | all-to-all | bytes 1048576 | tf_op jit(solution)/shard_map/blocks_exchange/all_to_all | solution.py:352
  63.1 0.1 split_shares.1
  63.2 12.6 %all_to_all.27.in_ref = bf16[4,16,256]{2,1,0:T(8,128)(2,1)S(1)} all-to-all(bf16[4,16,256]{2,1,0:T(8,128)(2,1)S(1)} %split_shares.1), channel_id=1, replica_groups={{0,4,8,12},{16,20,24,28},{32,36,40,44},{48,52,56,60},{64,68,72,76},{80,..., dimensions={0} | all-to-all | bytes 65536 | tf_op jit(solution)/shard_map/near_sum_exchange/all_to_all | solution.py:363
  75.8 21.4 %all_to_all.28.in_ref = bf16[8,16,256]{2,1,0:T(8,128)(2,1)S(1)} all-to-all(bf16[8,16,256]{2,1,0:T(8,128)(2,1)S(1)} %near_sum_exchange.1), channel_id=1, replica_groups={{0,16,32,48,256,272,288,304},{4,20,36,52,260,276,292,308},{8,24,40,56,2..., dimensions={0} | all-to-all | bytes 131072 | tf_op jit(solution)/shard_map/far_sum_exchange/all_to_all | solution.py:366
  97.2 0.7 far_sum_exchange.1
  97.8 5.3 %all-to-all-start.4 = ((bf16[16,16,256]{2,1,0:T(8,128)(2,1)}), bf16[16,16,256]{2,1,0:T(8,128)(2,1)S(1)}, u32[]{:S(2)}, u32[]{:S(2)}) async-start(bf16[16,16,256]{2,1,0:T(8,128)(2,1)} %far_sum_exchange.1), calls=%async_computation.4 | async-start | bytes 262144 | tf_op jit(solution)/shard_map/spread_exchange/all_to_all | solution.py:369
  103.2 1.0 place_outputs.1
  104.1 5.3 %all-to-all-done.4.refs_0_ = bf16[16,16,256]{2,1,0:T(8,128)(2,1)S(1)} async-done(((bf16[16,16,256]{2,1,0:T(8,128)(2,1)}), bf16[16,16,256]{2,1,0:T(8,128)(2,1)S(1)}, u32[]{:S(2)}, u32[]{:S(2)}) %all-to-all-start.4) | async-done | bytes 131104 | tf_op jit(solution)/shard_map/spread_exchange/all_to_all | solution.py:369
  109.4 0.7 finish.1
  (1 shorter events, 0.0 us)
Async XLA Ops:
  0.6 18.9 %copy-start = (bf16[16,1728]{1,0:T(8,128)(2,1)S(1)}, bf16[16,1728]{1,0:T(8,128)(2,1)}, u32[]{:S(2)}) copy-start(bf16[16,1728]{1,0:T(8,128)(2,1)} %first_ref.1) | copy-start | bytes 165892
  0.6 18.9 %copy-start.1 = (bf16[16,1728]{1,0:T(8,128)(2,1)S(1)}, bf16[16,1728]{1,0:T(8,128)(2,1)}, u32[]{:S(2)}) copy-start(bf16[16,1728]{1,0:T(8,128)(2,1)} %second_ref.1) | copy-start | bytes 165892
  1.5 18.1 %collective-permute-start = (bf16[256,128]{1,0:T(8,128)(2,1)S(1)}, bf16[256,128]{1,0:T(8,128)(2,1)S(1)}, u32[]{:S(2)}, u32[]{:S(2)}) collective-permute-start(bf16[256,128]{1,0:T(8,128)(2,1)S(1)} %pad_maximum_fusion.near_ref), channel_id=1, source_target_pairs={{0,256},{64,320},{128,384},{192,448},{256,0},{320,64},{384,128},{4... | collective-permute-start | bytes 196616 | tf_op jit(solution)/shard_map/halves_exchange/ppermute | solution.py:316
  37.4 8.7 %collective-permute-start.2 = (bf16[1024,128]{1,0:T(8,128)(2,1)S(1)}, bf16[1024,128]{1,0:T(8,128)(2,1)S(1)}, u32[]{:S(2)}, u32[]{:S(2)}) collective-permute-start(bf16[1024,128]{1,0:T(8,128)(2,1)S(1)} %unpack_windows.1.own_ref), channel_id=1, source_target_pairs={{0,316},{4,0},{8,4},{12,8},{16,12},{20,16},{24,20},{28,24},{32,28}... | collective-permute-start | bytes 786440 | tf_op jit(solution)/shard_map/z_rim_exchange/ppermute | solution.py:330
  41.8 4.3 %collective-permute-start.1 = (bf16[1024,128]{1,0:T(8,128)(2,1)S(1)}, bf16[1024,128]{1,0:T(8,128)(2,1)S(1)}, u32[]{:S(2)}, u32[]{:S(2)}) collective-permute-start(bf16[1024,128]{1,0:T(8,128)(2,1)S(1)} %unpack_windows.1.own_ref), channel_id=1, source_target_pairs={{0,4},{4,8},{8,12},{12,16},{16,20},{20,24},{24,28},{28,32},{32,36}... | collective-permute-start | bytes 786440 | tf_op jit(solution)/shard_map/z_rim_exchange/ppermute | solution.py:329
  97.8 11.6 %all-to-all-start.4 = ((bf16[16,16,256]{2,1,0:T(8,128)(2,1)}), bf16[16,16,256]{2,1,0:T(8,128)(2,1)S(1)}, u32[]{:S(2)}, u32[]{:S(2)}) async-start(bf16[16,16,256]{2,1,0:T(8,128)(2,1)} %far_sum_exchange.1), calls=%async_computation.4 | async-start | bytes 262144 | tf_op jit(solution)/shard_map/spread_exchange/all_to_all | solution.py:369

commit v4 on v3

--- a/solution.py
+++ b/solution.py
@@ -39,9 +39,9 @@
     [at_device(half, y, 2 * pair + odd, core) for odd in HALVES for core in CORES]
     for half in HALVES for y in range(SYH) for pair in PAIRS
 ]
-EIGHTS = [
-    [at_device(half, y, 2 * pair + odd, core) for half in HALVES for pair in PAIRS]
-    for y in range(SYH) for odd in HALVES for core in CORES
+FAR_FOURS = [
+    [at_device(half, y, 2 * pair + odd, core) for pair in PAIRS]
+    for half in HALVES for y in range(SYH) for odd in HALVES for core in CORES
 ]
 SIXTEENS = [
     [at_device(half, y, 2 * pair + odd, core) for y in range(SYH) for odd in HALVES for core in CORES]
@@ -249,12 +249,11 @@
             first = QUARTER + at * 64
             out_ref[to, :, first : first + 64] = flat[:, to * 64 : to * 64 + 64]
     for base, cells, source, at in ((0, cells_3, field, 3), (HALF, cells_2, act, 2)):
-        own = pl.ds(pl.multiple_of(half * 64, 64), 64)
-        flat = jnp.transpose(cells[:, own, :].reshape(256, 128))[0:C, :].astype(BF)
+        flat = jnp.transpose(cells[...].reshape(count, 128))[0:C, :].astype(BF)
         for b in range(3):
             for c in range(3):
-                near = pl.ds(pl.multiple_of((at + c) * Y + half * 64, 16), 64)
-                near = jnp.concatenate([source[at + b + z, near, :] for z in range(4)], axis=0)
+                near = slice((at + c) * Y, (at + c + XB) * Y)
+                near = jnp.concatenate([source[at + b + z, near, :] for z in range(ZB)], axis=0)
                 sums = jnp.dot(flat, near, preferred_element_type=F32).astype(BF)
                 for a in range(3):
                     first = base + tap_column(a, b, c)
@@ -361,9 +360,9 @@
         )
     with jax.named_scope("near_sum_exchange"):
         pieces = lax.all_to_all(pieces, PENCIL, 0, 0, tiled=True, axis_index_groups=FOURS)
-        pieces = call(sum_kernel, shape((8, 16, PIECE), BF), [], pieces)
+        pieces = call(sum_kernel, shape((4, 16, PIECE), BF), [], pieces)
     with jax.named_scope("far_sum_exchange"):
-        pieces = lax.all_to_all(pieces, PENCIL, 0, 0, tiled=True, axis_index_groups=EIGHTS)
+        pieces = lax.all_to_all(pieces, PENCIL, 0, 0, tiled=True, axis_index_groups=FAR_FOURS)
         pieces = call(sum_kernel, shape((16, 16, PIECE), BF), [], pieces)
     with jax.named_scope("spread_exchange"):
         pieces = lax.all_to_all(pieces, PENCIL, 0, 0, tiled=True, axis_index_groups=SIXTEENS)

time: 110 us -> 106 us (0.964)
  blocking collectives: 62.7 us -> 57.8 us
    all_to_all x1, blocking collectives: 21.4 us -> 16.5 us  [body(): lax.all_to_all(pieces, PENCIL, 0, 0, tiled=True, axis_index_groups=FAR_FO...]
where the time goes in v4:
time: 106 us
  blocking collectives  57.8 us (55%)
  starting transfers between devices  26.5 us (25%)
  waiting for transfers between devices  11.2 us (11%)
  Pallas kernels  8.84 us (8%)
    all_to_all x1, blocking collectives, body(): lax.all_to_all(packed, ('sy', 'filt'), 0, 0, tiled=True, axis_index_group...  16.9 us
    all_to_all x1, blocking collectives, body(): lax.all_to_all(pieces, PENCIL, 0, 0, tiled=True, axis_index_groups=FAR_FO...  16.5 us
    ppermute x1, starting transfers between devices, body(): far = lax.ppermute(near, 'sy', [(i, (i + SYH) % SY) for i in range(SY)])  16.3 us
    all_to_all x1, blocking collectives, body(): lax.all_to_all(pieces, PENCIL, 0, 0, tiled=True, axis_index_groups=FOURS)  12.6 us
    all_to_all x1, blocking collectives, body(): lax.all_to_all(shares, ('sy', 'filt'), 0, 0, tiled=True, axis_index_group...  11.7 us
    pallas_call x8, Pallas kernels, call(): pl.pallas_call(kernel, out_shape=out_shape, scratch_shapes=scratch, compi...  8.84 us
    all_to_all x1, starting transfers between devices, body(): lax.all_to_all(pieces, PENCIL, 0, 0, tiled=True, axis_index_groups=SIXTEENS)  5.5 us
    all_to_all x1, waiting for transfers between devices, body(): lax.all_to_all(pieces, PENCIL, 0, 0, tiled=True, axis_index_groups=SIXTEENS)  5.27 us
  transfers between devices with their start and end apart: 4, of which 3 were waited for; matrix products, arithmetic and copies ran while one was open for 0% of the time, Pallas kernels for 1%

profile of v4, /device:TPU:1, one launch (start us, length us, event | category | flops | bytes accessed | tf_op | source)
XLA Modules:
  0.0 105.7 jit_solution(6459356800442859733)
XLA Ops:
  0.6 0.0 copy-start
  0.6 0.0 copy-start.1
  0.7 0.8 pad_maximum_fusion.near_ref
  1.5 16.3 %collective-permute-start = (bf16[256,128]{1,0:T(8,128)(2,1)S(1)}, bf16[256,128]{1,0:T(8,128)(2,1)S(1)}, u32[]{:S(2)}, u32[]{:S(2)}) collective-permute-start(bf16[256,128]{1,0:T(8,128)(2,1)S(1)} %pad_maximum_fusion.near_ref), channel_id=1, source_target_pairs={{0,256},{64,320},{128,384},{192,448},{256,0},{320,64},{384,128},{4... | collective-permute-start | bytes 196616 | tf_op jit(solution)/shard_map/halves_exchange/ppermute | solution.py:315
  17.7 1.8 %collective-permute-done.far_ref = bf16[256,128]{1,0:T(8,128)(2,1)S(1)} collective-permute-done((bf16[256,128]{1,0:T(8,128)(2,1)S(1)}, bf16[256,128]{1,0:T(8,128)(2,1)S(1)}, u32[]{:S(2)}, u32[]{:S(2)}) %collective-permute-start) | collective-permute-done | bytes 65568 | tf_op jit(solution)/shard_map/halves_exchange/ppermute | solution.py:315
  19.6 0.0 copy-done
  19.6 0.0 copy-done.1
  19.6 0.7 pack_windows.1
  20.3 16.9 %all_to_all.25.in_ref.windows_ref = bf16[16,176,128]{2,1,0:T(8,128)(2,1)S(1)} all-to-all(bf16[16,176,128]{2,1,0:T(8,128)(2,1)S(1)} %pack_windows.1), channel_id=1, replica_groups={{0,1,2,3,64,65,66,67,128,129,130,131,192,193,194,195},{256,257,258,259,..., dimensions={0} | all-to-all | bytes 1441792 | tf_op jit(solution)/shard_map/windows_exchange/all_to_all | solution.py:324
  37.2 0.2 unpack_windows.1.own_ref
  37.4 4.4 %collective-permute-start.2 = (bf16[1024,128]{1,0:T(8,128)(2,1)S(1)}, bf16[1024,128]{1,0:T(8,128)(2,1)S(1)}, u32[]{:S(2)}, u32[]{:S(2)}) collective-permute-start(bf16[1024,128]{1,0:T(8,128)(2,1)S(1)} %unpack_windows.1.own_ref), channel_id=1, source_target_pairs={{0,316},{4,0},{8,4},{12,8},{16,12},{20,16},{24,20},{28,24},{32,28}... | collective-permute-start | bytes 786440 | tf_op jit(solution)/shard_map/z_rim_exchange/ppermute | solution.py:329
  41.8 0.3 collective-permute-start.1
  42.1 4.0 %collective-permute-done.2.above_ref = bf16[1024,128]{1,0:T(8,128)(2,1)S(1)} collective-permute-done((bf16[1024,128]{1,0:T(8,128)(2,1)S(1)}, bf16[1024,128]{1,0:T(8,128)(2,1)S(1)}, u32[]{:S(2)}, u32[]{:S(2)}) %collective-permute-start.2) | collective-permute-done | bytes 262176 | tf_op jit(solution)/shard_map/z_rim_exchange/ppermute | solution.py:329
  46.2 0.0 collective-permute-done.1.below_ref
  46.2 5.5 %layers.1 = bf16[4,64,1024]{2,1,0:T(8,128)(2,1)S(1)} custom-call(bf16[1024,128]{1,0:T(8,128)(2,1)S(1)} %collective-permute-done.1.below_ref, bf16[1024,128]{1,0:T(8,128)(2,1)S(1)} %unpack_windows.1.own_ref, bf16[1024,128]{1,0:T(8,128)(2,1)S(1)} %collective-permute-done.2.above_ref, bf16[16,176,128]{2,1,0:T(8,128)(2,1)S(1)} %all_to_all.25.in_ref.windows_ref), custom_call_target="tpu_custom_call" | custom-call | tf_op jit(solution)/shard_map/layers/pallas_call | solution.py:71
  51.7 11.7 %all_to_all.26.in_ref = bf16[16,16,1024]{2,1,0:T(8,128)(2,1)S(1)} all-to-all(bf16[16,16,1024]{2,1,0:T(8,128)(2,1)S(1)} %bitcast.5), channel_id=1, replica_groups={{0,1,2,3,64,65,66,67,128,129,130,131,192,193,194,195},{256,257,258,259,..., dimensions={0} | all-to-all | bytes 1048576 | tf_op jit(solution)/shard_map/blocks_exchange/all_to_all | solution.py:351
  63.4 0.1 split_shares.1
  63.5 12.6 %all_to_all.27.in_ref = bf16[4,16,256]{2,1,0:T(8,128)(2,1)S(1)} all-to-all(bf16[4,16,256]{2,1,0:T(8,128)(2,1)S(1)} %split_shares.1), channel_id=1, replica_groups={{0,4,8,12},{16,20,24,28},{32,36,40,44},{48,52,56,60},{64,68,72,76},{80,..., dimensions={0} | all-to-all | bytes 65536 | tf_op jit(solution)/shard_map/near_sum_exchange/all_to_all | solution.py:362
  76.1 16.5 %all_to_all.28.in_ref = bf16[4,16,256]{2,1,0:T(8,128)(2,1)S(1)} all-to-all(bf16[4,16,256]{2,1,0:T(8,128)(2,1)S(1)} %near_sum_exchange.1), channel_id=1, replica_groups={{0,16,32,48},{4,20,36,52},{8,24,40,56},{12,28,44,60},{64,80,96,112},{68..., dimensions={0} | all-to-all | bytes 65536 | tf_op jit(solution)/shard_map/far_sum_exchange/all_to_all | solution.py:365
  92.6 0.7 far_sum_exchange.1
  93.3 5.5 %all-to-all-start.4 = ((bf16[16,16,256]{2,1,0:T(8,128)(2,1)}), bf16[16,16,256]{2,1,0:T(8,128)(2,1)S(1)}, u32[]{:S(2)}, u32[]{:S(2)}) async-start(bf16[16,16,256]{2,1,0:T(8,128)(2,1)} %far_sum_exchange.1), calls=%async_computation.4 | async-start | bytes 262144 | tf_op jit(solution)/shard_map/spread_exchange/all_to_all | solution.py:368
  98.8 1.0 place_outputs.1
  99.8 5.3 %all-to-all-done.4.refs_0_ = bf16[16,16,256]{2,1,0:T(8,128)(2,1)S(1)} async-done(((bf16[16,16,256]{2,1,0:T(8,128)(2,1)}), bf16[16,16,256]{2,1,0:T(8,128)(2,1)S(1)}, u32[]{:S(2)}, u32[]{:S(2)}) %all-to-all-start.4) | async-done | bytes 131104 | tf_op jit(solution)/shard_map/spread_exchange/all_to_all | solution.py:368
  105.0 0.7 finish.1
  (1 shorter events, 0.0 us)
Async XLA Ops:
  0.6 18.9 %copy-start = (bf16[16,1728]{1,0:T(8,128)(2,1)S(1)}, bf16[16,1728]{1,0:T(8,128)(2,1)}, u32[]{:S(2)}) copy-start(bf16[16,1728]{1,0:T(8,128)(2,1)} %first_ref.1) | copy-start | bytes 165892
  0.6 18.9 %copy-start.1 = (bf16[16,1728]{1,0:T(8,128)(2,1)S(1)}, bf16[16,1728]{1,0:T(8,128)(2,1)}, u32[]{:S(2)}) copy-start(bf16[16,1728]{1,0:T(8,128)(2,1)} %second_ref.1) | copy-start | bytes 165892
  1.5 18.1 %collective-permute-start = (bf16[256,128]{1,0:T(8,128)(2,1)S(1)}, bf16[256,128]{1,0:T(8,128)(2,1)S(1)}, u32[]{:S(2)}, u32[]{:S(2)}) collective-permute-start(bf16[256,128]{1,0:T(8,128)(2,1)S(1)} %pad_maximum_fusion.near_ref), channel_id=1, source_target_pairs={{0,256},{64,320},{128,384},{192,448},{256,0},{320,64},{384,128},{4... | collective-permute-start | bytes 196616 | tf_op jit(solution)/shard_map/halves_exchange/ppermute | solution.py:315
  37.4 8.7 %collective-permute-start.2 = (bf16[1024,128]{1,0:T(8,128)(2,1)S(1)}, bf16[1024,128]{1,0:T(8,128)(2,1)S(1)}, u32[]{:S(2)}, u32[]{:S(2)}) collective-permute-start(bf16[1024,128]{1,0:T(8,128)(2,1)S(1)} %unpack_windows.1.own_ref), channel_id=1, source_target_pairs={{0,316},{4,0},{8,4},{12,8},{16,12},{20,16},{24,20},{28,24},{32,28}... | collective-permute-start | bytes 786440 | tf_op jit(solution)/shard_map/z_rim_exchange/ppermute | solution.py:329
  41.8 4.3 %collective-permute-start.1 = (bf16[1024,128]{1,0:T(8,128)(2,1)S(1)}, bf16[1024,128]{1,0:T(8,128)(2,1)S(1)}, u32[]{:S(2)}, u32[]{:S(2)}) collective-permute-start(bf16[1024,128]{1,0:T(8,128)(2,1)S(1)} %unpack_windows.1.own_ref), channel_id=1, source_target_pairs={{0,4},{4,8},{8,12},{12,16},{16,20},{20,24},{24,28},{28,32},{32,36}... | collective-permute-start | bytes 786440 | tf_op jit(solution)/shard_map/z_rim_exchange/ppermute | solution.py:328
  93.3 11.7 %all-to-all-start.4 = ((bf16[16,16,256]{2,1,0:T(8,128)(2,1)}), bf16[16,16,256]{2,1,0:T(8,128)(2,1)S(1)}, u32[]{:S(2)}, u32[]{:S(2)}) async-start(bf16[16,16,256]{2,1,0:T(8,128)(2,1)} %far_sum_exchange.1), calls=%async_computation.4 | async-start | bytes 262144 | tf_op jit(solution)/shard_map/spread_exchange/all_to_all | solution.py:368

commit v5 on v4

--- a/solution.py
+++ b/solution.py
@@ -23,7 +23,6 @@
 GRADS = 2 * HALF
 QUARTER = GRADS // SYH
 PIECE = 256
-TILES = HALF // (SYH // 2) // 128
 COLUMNS = 27 * C
 PARAMS = pltpu.CompilerParams(vmem_limit_bytes=48 * 1024 * 1024)
 
@@ -73,16 +72,7 @@
     )(*args)
 
 
-def pack_kernel(near_ref, far_ref, first_ref, second_ref, out_ref, held, filters):
-    filters[...] = jnp.zeros_like(filters)
-    filters[:, 0:COLUMNS] = first_ref[...]
-    filters[:, HALF : HALF + COLUMNS] = second_ref[...]
-    share = lax.axis_index("sy") % SYH
-    for tile in range(TILES):
-        first = pl.multiple_of((share * TILES + tile) * 128, 128)
-        columns = filters[:, pl.ds(first, 128)]
-        for k in range(BLOCKS):
-            out_ref[k, 64 + 16 * tile : 80 + 16 * tile, :] = columns
+def pack_kernel(near_ref, far_ref, out_ref, held):
     lower = lax.axis_index("sy") < SYH
     near, far = near_ref[...].astype(F32), far_ref[...].astype(F32)
     held[0:256, :] = jnp.where(lower, near, far)
@@ -93,7 +83,7 @@
         total = turned(rows[0], RIM - XB * k)
         for yz in range(1, 8):
             total = jnp.where(slot == yz, turned(rows[yz], 16 * yz + RIM - XB * k), total)
-        out_ref[k, 0:64, :] = total.astype(BF)
+        out_ref[k] = total.astype(BF)
 
 
 def unpack_kernel(in_ref, out_ref, held):
@@ -129,6 +119,14 @@
     ref[z, :, 128:256] = after.astype(BF)
 
 
+def store_field(ref, at, slab_ref, z):
+    x = slab_ref[z * PLANE : (z + 1) * PLANE, :].astype(F32)
+    before, after = y_taps(x)
+    low = lanes_of(x.shape) < C
+    ref[at, :, 0:128] = jnp.where(low, before, turned(x, C)).astype(BF)
+    ref[at, :, 128:256] = after.astype(BF)
+
+
 def softplus(x):
     return jnp.maximum(x, 0.0) + jnp.log1p(jnp.exp(-jnp.abs(x)))
 
@@ -142,14 +140,12 @@
     return (9 * a + 3 * b + c) * C
 
 
-def filter_block(windows_ref, layer, f, a, b, c):
-    column = layer * HALF + tap_column(a, b, c)
-    tile = column // 128
-    top = 64 + 16 * (tile % TILES)
-    return windows_ref[(tile // TILES) * FILT + f, top : top + 16, column % 128 : column % 128 + C]
-
-
-def fill_forward(ref, windows_ref, layer):
+def filter_block(filters_ref, layer, f, a, b, c):
+    first = tap_column(a, b, c)
+    return filters_ref[f, layer, :, first : first + C]
+
+
+def fill_forward(ref, filters_ref, layer):
     ref[...] = jnp.zeros_like(ref)
     for b in range(3):
         for a in range(3):
@@ -157,11 +153,11 @@
                 for f in range(FILT):
                     row = at * C + f * 16
                     ref[row : row + 16, b * 256 + a * C : b * 256 + a * C + C] = filter_block(
-                        windows_ref, layer, f, a, b, c
+                        filters_ref, layer, f, a, b, c
                     )
 
 
-def fill_backward(ref, windows_ref, layer):
+def fill_backward(ref, filters_ref, layer):
     ref[...] = jnp.zeros_like(ref)
     for b in range(3):
         for a in range(3):
@@ -169,13 +165,21 @@
                 for f in range(FILT):
                     row = b * 256 + a * C + f * 16
                     ref[row : row + 16, at * C : at * C + C] = filter_block(
-                        windows_ref, layer, f, 2 - a, 2 - b, 2 - c
+                        filters_ref, layer, f, 2 - a, 2 - b, 2 - c
                     )
 
 
-def convolved(taps_ref, weights, z, wide, transposed):
-    rows = wide * Y
-    planes = jnp.concatenate([taps_ref[z + b, 0:rows, :] for b in range(3)], axis=1)
+def prepare_kernel(own_ref, filters_ref, weights, weights_t, field):
+    for layer in range(2):
+        fill_forward(weights.at[layer], filters_ref, layer)
+        fill_backward(weights_t.at[layer], filters_ref, layer)
+    for z in range(ZB):
+        store_field(field, z, own_ref, z)
+
+
+def convolved(planes, weights, transposed):
+    rows = planes[0].shape[0]
+    planes = jnp.concatenate(planes, axis=1)
     dims = (((1,), (1 if transposed else 0,)), ((), ()))
     sums = lax.dot_general(planes, weights, dims, preferred_element_type=F32)
     left, right = sums[:, 0:128], sums[:, 128:256]
@@ -193,8 +197,8 @@
 
 
 def main_kernel(
-    below_ref, own_ref, above_ref, windows_ref, out_ref,
-    field, act, delta_2, delta_1, pre_1, cells_0, cells_1, cells_2, cells_3, weights, weights_t,
+    below_ref, own_ref, above_ref, weights, weights_t, field_own, out_ref,
+    field, act, delta_2, delta_1, pre_1, cells_0, cells_1, cells_2, cells_3,
 ):
     half = lax.axis_index("sy") // SYH
     slabs = (below_ref, own_ref, above_ref)
@@ -203,21 +207,23 @@
         start = (z % ZB) * PLANE + first
         return slabs[z // ZB][start : start + count, :].astype(F32)
 
-    for layer in range(2):
-        fill_forward(weights.at[layer], windows_ref, layer)
-        fill_backward(weights_t.at[layer], windows_ref, layer)
-    for z in range(12):
-        x = slab_rows(z, 0, PLANE)
-        before, after = y_taps(x)
-        low = lanes_of(x.shape) < C
-        field[z, :, 0:128] = jnp.where(low, before, turned(x, C)).astype(BF)
-        field[z, :, 128:256] = after.astype(BF)
+    def field_rows(z, rows):
+        if ZB <= z < 2 * ZB:
+            return field_own[z - ZB, rows, :]
+        return field[z if z < ZB else z - ZB, rows, :]
+
+    def planes(ref, z):
+        return [ref[z + b] for b in range(3)]
+
+    for z in range(ZB):
+        store_field(field, z, below_ref, z)
+        store_field(field, ZB + z, above_ref, z)
     for z in range(10):
-        pre = convolved(field, weights[0], z, XW, True)
+        pre = convolved([field_rows(z + b, slice(0, PLANE)) for b in range(3)], weights[0], True)
         pre_1[z] = pre
         store_taps(act, z, softplus(pre).astype(BF).astype(F32))
     for z in range(8):
-        pre = convolved(act, weights[1], z, XW - 2, True)
+        pre = convolved(planes(act, z), weights[1], True)
         cotangent = slab_rows(z + 2, 2 * Y, (XW - 4) * Y)
         low = lanes_of(cotangent.shape) < C
         cotangent = jnp.where(low, turned(cotangent, C), cotangent)
@@ -227,13 +233,13 @@
             cells_0[z - 2] = softplus(pre[2 * Y : (2 + XB) * Y])
             cells_2[z - 2] = delta[2 * Y : (2 + XB) * Y]
     for z in range(6):
-        back = convolved(delta_2, weights_t[1], z, XW - 4, False)
+        back = convolved(planes(delta_2, z), weights_t[1], False)
         delta = (back * sigmoid(pre_1[z + 2, 2 * Y : (XW - 4) * Y, :])).astype(BF).astype(F32)
         store_taps(delta_1, z, delta)
         if 1 <= z < 5:
             cells_3[z - 1] = delta[Y : (1 + XB) * Y]
     for z in range(4):
-        cells_1[z] = convolved(delta_1, weights_t[0], z, XW - 6, False)
+        cells_1[z] = convolved(planes(delta_1, z), weights_t[0], False)
 
     count = ZB * XB * Y
     row = lax.broadcasted_iota(jnp.int32, (count, count // 2), 0)
@@ -248,12 +254,15 @@
         for to in range(SYH):
             first = QUARTER + at * 64
             out_ref[to, :, first : first + 64] = flat[:, to * 64 : to * 64 + 64]
-    for base, cells, source, at in ((0, cells_3, field, 3), (HALF, cells_2, act, 2)):
+    def act_rows(z, rows):
+        return act[z, rows, :]
+
+    for base, cells, source, at in ((0, cells_3, field_rows, 3), (HALF, cells_2, act_rows, 2)):
         flat = jnp.transpose(cells[...].reshape(count, 128))[0:C, :].astype(BF)
         for b in range(3):
             for c in range(3):
                 near = slice((at + c) * Y, (at + c + XB) * Y)
-                near = jnp.concatenate([source[at + b + z, near, :] for z in range(ZB)], axis=0)
+                near = jnp.concatenate([source(at + b + z, near) for z in range(ZB)], axis=0)
                 sums = jnp.dot(flat, near, preferred_element_type=F32).astype(BF)
                 for a in range(3):
                     first = base + tap_column(a, b, c)
@@ -264,7 +273,7 @@
         )
 
 
-def split_kernel(in_ref, out_ref):
+def split_kernel(in_ref, out_ref, result_ref, grad_input_ref, held):
     for to in range(4):
         wide = min(PIECE, QUARTER - to * PIECE)
         lanes = slice(to * PIECE, to * PIECE + wide)
@@ -274,19 +283,20 @@
         out_ref[to, :, 0:wide] = total.astype(BF)
         if wide < PIECE:
             out_ref[to, :, wide:PIECE] = jnp.zeros((16, PIECE - wide), BF)
-
-
-def outputs_kernel(in_ref, result_ref, grad_input_ref, held):
     blocks = [in_ref[k, :, QUARTER : QUARTER + 128].astype(F32) for k in range(BLOCKS)]
     slot = lanes_of((16, 128)) // XB
+    for bit in (1, 2, 4, 8):
+        clear = slot & bit == 0
+        blocks = [
+            jnp.where(clear, turned(blocks[k - bit], -bit * XB), blocks[k])
+            if k & bit
+            else jnp.where(clear, blocks[k], turned(blocks[k + bit], bit * XB))
+            for k in range(BLOCKS)
+        ]
     for at, ref in enumerate((result_ref, grad_input_ref)):
         for z in range(ZB):
             for yy in range(2):
-                first = at * 64 + z * 16 + yy * XB
-                total = turned(blocks[0], -first)
-                for k in range(1, BLOCKS):
-                    total = jnp.where(slot == k, turned(blocks[k], k * XB - first), total)
-                held[at, pl.ds(yy * ZB + z, 16, stride=8), :] = total
+                held[at, pl.ds(yy * ZB + z, 16, stride=8), :] = blocks[at * 8 + z * 2 + yy]
         ref[...] = held[at].astype(BF)
 
 
@@ -314,12 +324,17 @@
         near = jnp.concatenate([volume.reshape(128, 128), cotangent.reshape(128, 128)], axis=0)
         far = lax.ppermute(near, "sy", [(i, (i + SYH) % SY) for i in range(SY)])
     with jax.named_scope("pack_windows"):
-        packed = call(
+        packed = pl.pallas_call(
             pack_kernel,
-            shape((BLOCKS, 64 + 16 * TILES, 128), BF),
-            [pltpu.VMEM((512, 128), F32), pltpu.VMEM((16, 2 * HALF), BF)],
-            near, far, first_filters, second_filters,
-        )
+            out_shape=shape((BLOCKS, 64, 128), BF),
+            scratch_shapes=[pltpu.VMEM((512, 128), F32)],
+            compiler_params=PARAMS,
+            cost_estimate=pl.CostEstimate(flops=40_000_000_000, bytes_accessed=1_000_000, transcendentals=0),
+        )(near, far)
+    with jax.named_scope("filters_exchange"):
+        filters = jnp.broadcast_to(jnp.stack([first_filters, second_filters]), (FILT, 2, 16, COLUMNS))
+        filters = lax.all_to_all(filters, "filt", 0, 0, tiled=True)
+        packed, filters = lax.optimization_barrier((packed, filters))
     with jax.named_scope("windows_exchange"):
         windows = lax.all_to_all(packed, ("sy", "filt"), 0, 0, tiled=True, axis_index_groups=SAME_HALF)
     with jax.named_scope("unpack_windows"):
@@ -327,12 +342,19 @@
     with jax.named_scope("z_rim_exchange"):
         below = lax.ppermute(own, PENCIL, along_z(1))
         above = lax.ppermute(own, PENCIL, along_z(-1))
+    with jax.named_scope("prepare"):
+        weights, weights_t, field_own = call(
+            prepare_kernel,
+            (shape((2, 256, 768), BF), shape((2, 768, 256), BF), shape((ZB, PLANE, 256), BF)),
+            [],
+            own, filters,
+        )
     with jax.named_scope("layers"):
         partial = call(
             main_kernel,
             shape((SYH, C, QUARTER + 128), BF),
             [
-                pltpu.VMEM((12, XW * Y, 256), BF),
+                pltpu.VMEM((8, XW * Y, 256), BF),
                 pltpu.VMEM((10, (XW - 2) * Y, 256), BF),
                 pltpu.VMEM((8, (XW - 4) * Y, 256), BF),
                 pltpu.VMEM((6, (XW - 6) * Y, 256), BF),
@@ -341,20 +363,16 @@
                 pltpu.VMEM((ZB, XB * Y, 128), F32),
                 pltpu.VMEM((ZB, XB * Y, 128), F32),
                 pltpu.VMEM((ZB, XB * Y, 128), F32),
-                pltpu.VMEM((2, 256, 768), BF),
-                pltpu.VMEM((2, 768, 256), BF),
             ],
-            below, own, above, windows,
+            below, own, above, weights, weights_t, field_own,
         )
     with jax.named_scope("blocks_exchange"):
         shares = partial.reshape(BLOCKS, 16, QUARTER + 128)
         shares = lax.all_to_all(shares, ("sy", "filt"), 0, 0, tiled=True, axis_index_groups=SAME_HALF)
     with jax.named_scope("split_shares"):
-        pieces = call(split_kernel, shape((4, 16, PIECE), BF), [], shares)
-    with jax.named_scope("place_outputs"):
-        result, grad_input = call(
-            outputs_kernel,
-            (shape((128, 128), BF), shape((128, 128), BF)),
+        pieces, result, grad_input = call(
+            split_kernel,
+            (shape((4, 16, PIECE), BF), shape((128, 128), BF), shape((128, 128), BF)),
             [pltpu.VMEM((2, 128, 128), F32)],
             shares,
         )

time: 106 us -> 102 us (0.962)
  starting transfers between devices: 26.5 us -> 24.7 us
  blocking collectives: 57.8 us -> 56.3 us
    all_to_all x0 -> x1, blocking collectives: none -> 10.8 us  [body(): lax.all_to_all(pieces, PENCIL, 0, 0, tiled=True, axis_index_groups=SIXTEENS)]
    all_to_all x1, blocking collectives: 16.9 us -> 12.4 us  [body(): lax.all_to_all(packed, ('sy', 'filt'), 0, 0, tiled=True, axis_index_group...]
    all_to_all x1, blocking collectives: 16.5 us -> 12.5 us  [body(): lax.all_to_all(pieces, PENCIL, 0, 0, tiled=True, axis_index_groups=FAR_FO...]
    all_to_all x1, blocking collectives: 12.6 us -> 8.66 us  [body(): lax.all_to_all(pieces, PENCIL, 0, 0, tiled=True, axis_index_groups=FOURS)]
    ppermute x1, waiting for transfers between devices: 1.85 us -> 0.01 us  [body(): far = lax.ppermute(near, 'sy', [(i, (i + SYH) % SY) for i in range(SY)])]
    all_to_all x1, starting transfers between devices: 5.5 us -> 4.01 us  [body(): filters = lax.all_to_all(filters, 'filt', 0, 0, tiled=True)]
    pallas_call x8 -> x7, Pallas kernels: 8.84 us -> 7.47 us  [call(): pl.pallas_call(kernel, out_shape=out_shape, scratch_shapes=scratch, compi...]
    all_to_all x1, waiting for transfers between devices: 5.27 us -> 6.62 us  [body(): filters = lax.all_to_all(filters, 'filt', 0, 0, tiled=True)]
  transfers between devices with their start and end apart: 4 -> 4, of which waited for: 3 -> 2; matrix products, arithmetic and copies ran while one was open for 0% -> 1% of each run, Pallas kernels for 1% -> 1%
where the time goes in v5:
time: 102 us
  blocking collectives  56.3 us (55%)
  starting transfers between devices  24.7 us (24%)
  waiting for transfers between devices  10.2 us (10%)
  Pallas kernels  8.11 us (8%)
    ppermute x1, starting transfers between devices, body(): far = lax.ppermute(near, 'sy', [(i, (i + SYH) % SY) for i in range(SY)])  16.3 us
    all_to_all x1, blocking collectives, body(): lax.all_to_all(pieces, PENCIL, 0, 0, tiled=True, axis_index_groups=FAR_FO...  12.5 us
    all_to_all x1, blocking collectives, body(): lax.all_to_all(packed, ('sy', 'filt'), 0, 0, tiled=True, axis_index_group...  12.4 us
    all_to_all x1, blocking collectives, body(): lax.all_to_all(shares, ('sy', 'filt'), 0, 0, tiled=True, axis_index_group...  12 us
    all_to_all x1, blocking collectives, body(): lax.all_to_all(pieces, PENCIL, 0, 0, tiled=True, axis_index_groups=SIXTEENS)  10.8 us
    all_to_all x1, blocking collectives, body(): lax.all_to_all(pieces, PENCIL, 0, 0, tiled=True, axis_index_groups=FOURS)  8.66 us
    pallas_call x7, Pallas kernels, call(): pl.pallas_call(kernel, out_shape=out_shape, scratch_shapes=scratch, compi...  7.47 us
    all_to_all x1, waiting for transfers between devices, body(): filters = lax.all_to_all(filters, 'filt', 0, 0, tiled=True)  6.62 us
  transfers between devices with their start and end apart: 4, of which 2 were waited for; matrix products, arithmetic and copies ran while one was open for 1% of the time, Pallas kernels for 1%

profile of v5, /device:TPU:1, one launch (start us, length us, event | category | flops | bytes accessed | tf_op | source)
XLA Modules:
  0.0 101.6 jit_solution(5402452048489130561)
XLA Ops:
  0.6 0.0 copy-start
  0.6 0.0 copy-start.1
  0.7 0.8 pad_maximum_fusion.1.near_ref
  1.5 16.3 %collective-permute-start = (bf16[256,128]{1,0:T(8,128)(2,1)S(1)}, bf16[256,128]{1,0:T(8,128)(2,1)S(1)}, u32[]{:S(2)}, u32[]{:S(2)}) collective-permute-start(bf16[256,128]{1,0:T(8,128)(2,1)S(1)} %pad_maximum_fusion.1.near_ref), channel_id=1, source_target_pairs={{0,256},{64,320},{128,384},{192,448},{256,0},{320,64},{384,128},{4... | collective-permute-start | bytes 196616 | tf_op jit(solution)/shard_map/halves_exchange/ppermute | solution.py:325
  17.7 0.0 copy-done
  17.8 0.8 broadcast_in_dim.3
  18.6 4.0 %all-to-all-start = ((bf16[4,2,16,1728]{3,2,1,0:T(8,128)(2,1)}), bf16[4,2,16,1728]{3,2,1,0:T(8,128)(2,1)S(1)}, u32[]{:S(2)}, u32[]{:S(2)}) async-start(bf16[4,2,16,1728]{3,2,1,0:T(8,128)(2,1)} %broadcast_in_dim.3), calls=%async_computation | async-start | bytes 917504 | tf_op jit(solution)/shard_map/filters_exchange/all_to_all | solution.py:336
  22.6 0.0 collective-permute-done.far_ref
  22.6 0.6 pack_windows.1
  23.2 6.6 %all-to-all-done.filters_ref = bf16[4,2,16,1728]{3,2,1,0:T(8,128)(2,1)S(1)} async-done(((bf16[4,2,16,1728]{3,2,1,0:T(8,128)(2,1)}), bf16[4,2,16,1728]{3,2,1,0:T(8,128)(2,1)S(1)}, u32[]{:S(2)}, u32[]{:S(2)}) %all-to-all-start) | async-done | bytes 442400 | tf_op jit(solution)/shard_map/filters_exchange/all_to_all | solution.py:336
  29.9 12.4 %all_to_all.30.in_ref = bf16[16,64,128]{2,1,0:T(8,128)(2,1)S(1)} all-to-all(bf16[16,64,128]{2,1,0:T(8,128)(2,1)S(1)} %pack_windows.1), channel_id=1, replica_groups={{0,1,2,3,64,65,66,67,128,129,130,131,192,193,194,195},{256,257,258,259,..., dimensions={0} | all-to-all | bytes 524288 | tf_op jit(solution)/shard_map/windows_exchange/all_to_all | solution.py:339
  42.2 0.2 unpack_windows.1.own_ref
  42.5 3.8 %collective-permute-start.2 = (bf16[1024,128]{1,0:T(8,128)(2,1)S(1)}, bf16[1024,128]{1,0:T(8,128)(2,1)S(1)}, u32[]{:S(2)}, u32[]{:S(2)}) collective-permute-start(bf16[1024,128]{1,0:T(8,128)(2,1)S(1)} %unpack_windows.1.own_ref), channel_id=1, source_target_pairs={{0,316},{4,0},{8,4},{12,8},{16,12},{20,16},{24,20},{28,24},{32,28}... | collective-permute-start | bytes 786440 | tf_op jit(solution)/shard_map/z_rim_exchange/ppermute | solution.py:344
  46.2 0.6 collective-permute-start.1
  46.9 0.8 prepare.1
  47.7 3.5 %collective-permute-done.2.above_ref = bf16[1024,128]{1,0:T(8,128)(2,1)S(1)} collective-permute-done((bf16[1024,128]{1,0:T(8,128)(2,1)S(1)}, bf16[1024,128]{1,0:T(8,128)(2,1)S(1)}, u32[]{:S(2)}, u32[]{:S(2)}) %collective-permute-start.2) | collective-permute-done | bytes 262176 | tf_op jit(solution)/shard_map/z_rim_exchange/ppermute | solution.py:344
  51.2 0.0 collective-permute-done.1.below_ref
  51.2 4.8 %layers.1 = bf16[4,64,1024]{2,1,0:T(8,128)(2,1)S(1)} custom-call(bf16[1024,128]{1,0:T(8,128)(2,1)S(1)} %collective-permute-done.1.below_ref, bf16[1024,128]{1,0:T(8,128)(2,1)S(1)} %unpack_windows.1.own_ref, bf16[1024,128]{1,0:T(8,128)(2,1)S(1)} %collective-permute-done.2.above_ref, bf16[2,256,768]{2,1,0:T(8,128)(2,1)S(1)} %get-tuple-element.16.weights, ...), custom_call_target="tpu_custom_call" | custom-call | tf_op jit(solution)/shard_map/layers/pallas_call | solution.py:70
  56.0 12.0 %all_to_all.31.in_ref = bf16[16,16,1024]{2,1,0:T(8,128)(2,1)S(1)} all-to-all(bf16[16,16,1024]{2,1,0:T(8,128)(2,1)S(1)} %bitcast.7), channel_id=1, replica_groups={{0,1,2,3,64,65,66,67,128,129,130,131,192,193,194,195},{256,257,258,259,..., dimensions={0} | all-to-all | bytes 1048576 | tf_op jit(solution)/shard_map/blocks_exchange/all_to_all | solution.py:371
  68.0 0.9 split_shares.1
  68.9 8.7 %all_to_all.32.in_ref = bf16[4,16,256]{2,1,0:T(8,128)(2,1)S(1)} all-to-all(bf16[4,16,256]{2,1,0:T(8,128)(2,1)S(1)} %get-tuple-element.21), channel_id=1, replica_groups={{0,4,8,12},{16,20,24,28},{32,36,40,44},{48,52,56,60},{64,68,72,76},{80,..., dimensions={0} | all-to-all | bytes 65536 | tf_op jit(solution)/shard_map/near_sum_exchange/all_to_all | solution.py:380
  77.6 12.5 %all_to_all.33.in_ref = bf16[4,16,256]{2,1,0:T(8,128)(2,1)S(1)} all-to-all(bf16[4,16,256]{2,1,0:T(8,128)(2,1)S(1)} %near_sum_exchange.1), channel_id=1, replica_groups={{0,16,32,48},{4,20,36,52},{8,24,40,56},{12,28,44,60},{64,80,96,112},{68..., dimensions={0} | all-to-all | bytes 65536 | tf_op jit(solution)/shard_map/far_sum_exchange/all_to_all | solution.py:383
  90.1 10.8 %all_to_all.34.refs_0_ = bf16[16,16,256]{2,1,0:T(8,128)(2,1)S(1)} all-to-all(bf16[16,16,256]{2,1,0:T(8,128)(2,1)S(1)} %far_sum_exchange.1), channel_id=1, replica_groups={{0,4,8,12,64,68,72,76,128,132,136,140,192,196,200,204},{16,20,24,28,80,..., dimensions={0} | all-to-all | bytes 262144 | tf_op jit(solution)/shard_map/spread_exchange/all_to_all | solution.py:386
  100.9 0.7 finish.1
  (4 shorter events, 0.0 us)
Async XLA Ops:
  0.6 17.1 %copy-start = (bf16[16,1728]{1,0:T(8,128)(2,1)S(1)}, bf16[16,1728]{1,0:T(8,128)(2,1)}, u32[]{:S(2)}) copy-start(bf16[16,1728]{1,0:T(8,128)(2,1)} %param.6) | copy-start | bytes 165892
  0.6 17.1 %copy-start.1 = (bf16[16,1728]{1,0:T(8,128)(2,1)S(1)}, bf16[16,1728]{1,0:T(8,128)(2,1)}, u32[]{:S(2)}) copy-start(bf16[16,1728]{1,0:T(8,128)(2,1)} %param.5) | copy-start | bytes 165892
  1.5 21.1 %collective-permute-start = (bf16[256,128]{1,0:T(8,128)(2,1)S(1)}, bf16[256,128]{1,0:T(8,128)(2,1)S(1)}, u32[]{:S(2)}, u32[]{:S(2)}) collective-permute-start(bf16[256,128]{1,0:T(8,128)(2,1)S(1)} %pad_maximum_fusion.1.near_ref), channel_id=1, source_target_pairs={{0,256},{64,320},{128,384},{192,448},{256,0},{320,64},{384,128},{4... | collective-permute-start | bytes 196616 | tf_op jit(solution)/shard_map/halves_exchange/ppermute | solution.py:325
  18.6 11.3 %all-to-all-start = ((bf16[4,2,16,1728]{3,2,1,0:T(8,128)(2,1)}), bf16[4,2,16,1728]{3,2,1,0:T(8,128)(2,1)S(1)}, u32[]{:S(2)}, u32[]{:S(2)}) async-start(bf16[4,2,16,1728]{3,2,1,0:T(8,128)(2,1)} %broadcast_in_dim.3), calls=%async_computation | async-start | bytes 917504 | tf_op jit(solution)/shard_map/filters_exchange/all_to_all | solution.py:336
  42.5 8.7 %collective-permute-start.2 = (bf16[1024,128]{1,0:T(8,128)(2,1)S(1)}, bf16[1024,128]{1,0:T(8,128)(2,1)S(1)}, u32[]{:S(2)}, u32[]{:S(2)}) collective-permute-start(bf16[1024,128]{1,0:T(8,128)(2,1)S(1)} %unpack_windows.1.own_ref), channel_id=1, source_target_pairs={{0,316},{4,0},{8,4},{12,8},{16,12},{20,16},{24,20},{28,24},{32,28}... | collective-permute-start | bytes 786440 | tf_op jit(solution)/shard_map/z_rim_exchange/ppermute | solution.py:344
  46.2 5.0 %collective-permute-start.1 = (bf16[1024,128]{1,0:T(8,128)(2,1)S(1)}, bf16[1024,128]{1,0:T(8,128)(2,1)S(1)}, u32[]{:S(2)}, u32[]{:S(2)}) collective-permute-start(bf16[1024,128]{1,0:T(8,128)(2,1)S(1)} %unpack_windows.1.own_ref), channel_id=1, source_target_pairs={{0,4},{4,8},{8,12},{12,16},{16,20},{20,24},{24,28},{28,32},{32,36}... | collective-permute-start | bytes 786440 | tf_op jit(solution)/shard_map/z_rim_exchange/ppermute | solution.py:343

commit v6 on v5

--- a/solution.py
+++ b/solution.py
@@ -273,7 +273,7 @@
         )
 
 
-def split_kernel(in_ref, out_ref, result_ref, grad_input_ref, held):
+def split_kernel(in_ref, out_ref):
     for to in range(4):
         wide = min(PIECE, QUARTER - to * PIECE)
         lanes = slice(to * PIECE, to * PIECE + wide)
@@ -283,7 +283,24 @@
         out_ref[to, :, 0:wide] = total.astype(BF)
         if wide < PIECE:
             out_ref[to, :, wide:PIECE] = jnp.zeros((16, PIECE - wide), BF)
-    blocks = [in_ref[k, :, QUARTER : QUARTER + 128].astype(F32) for k in range(BLOCKS)]
+
+
+def sum_kernel(in_ref, out_ref):
+    total = in_ref[0].astype(F32)
+    for k in range(1, in_ref.shape[0]):
+        total = total + in_ref[k].astype(F32)
+    total = total.astype(BF)
+    for k in range(out_ref.shape[0]):
+        out_ref[k] = total
+
+
+def finish_kernel(factor, in_ref, shares_ref, result_ref, grad_input_ref, first_ref, second_ref, held):
+    for base, ref in ((0, first_ref), (8, second_ref)):
+        for k in range(8):
+            first = (k // 4) * QUARTER + (k % 4) * PIECE
+            wide = min(PIECE, QUARTER - (k % 4) * PIECE, COLUMNS - first)
+            ref[:, first : first + wide] = in_ref[base + k, :, 0:wide].astype(F32) * factor
+    blocks = [shares_ref[k, :, QUARTER : QUARTER + 128].astype(F32) for k in range(BLOCKS)]
     slot = lanes_of((16, 128)) // XB
     for bit in (1, 2, 4, 8):
         clear = slot & bit == 0
@@ -298,23 +315,6 @@
             for yy in range(2):
                 held[at, pl.ds(yy * ZB + z, 16, stride=8), :] = blocks[at * 8 + z * 2 + yy]
         ref[...] = held[at].astype(BF)
-
-
-def sum_kernel(in_ref, out_ref):
-    total = in_ref[0].astype(F32)
-    for k in range(1, in_ref.shape[0]):
-        total = total + in_ref[k].astype(F32)
-    total = total.astype(BF)
-    for k in range(out_ref.shape[0]):
-        out_ref[k] = total
-
-
-def finish_kernel(factor, in_ref, first_ref, second_ref):
-    for base, ref in ((0, first_ref), (8, second_ref)):
-        for k in range(8):
-            first = (k // 4) * QUARTER + (k % 4) * PIECE
-            wide = min(PIECE, QUARTER - (k % 4) * PIECE, COLUMNS - first)
-            ref[:, first : first + wide] = in_ref[base + k, :, 0:wide].astype(F32) * factor
 
 
 def body(volume, first_filters, second_filters, cotangent):
@@ -370,12 +370,7 @@
         shares = partial.reshape(BLOCKS, 16, QUARTER + 128)
         shares = lax.all_to_all(shares, ("sy", "filt"), 0, 0, tiled=True, axis_index_groups=SAME_HALF)
     with jax.named_scope("split_shares"):
-        pieces, result, grad_input = call(
-            split_kernel,
-            (shape((4, 16, PIECE), BF), shape((128, 128), BF), shape((128, 128), BF)),
-            [pltpu.VMEM((2, 128, 128), F32)],
-            shares,
-        )
+        pieces = call(split_kernel, shape((4, 16, PIECE), BF), [], shares)
     with jax.named_scope("near_sum_exchange"):
         pieces = lax.all_to_all(pieces, PENCIL, 0, 0, tiled=True, axis_index_groups=FOURS)
         pieces = call(sum_kernel, shape((4, 16, PIECE), BF), [], pieces)
@@ -385,11 +380,14 @@
     with jax.named_scope("spread_exchange"):
         pieces = lax.all_to_all(pieces, PENCIL, 0, 0, tiled=True, axis_index_groups=SIXTEENS)
     with jax.named_scope("finish"):
-        first_grad, second_grad = call(
+        result, grad_input, first_grad, second_grad = call(
             lambda *refs: finish_kernel(factor, *refs),
-            (shape((16, COLUMNS), F32), shape((16, COLUMNS), F32)),
-            [],
-            pieces,
+            (
+                shape((128, 128), BF), shape((128, 128), BF),
+                shape((16, COLUMNS), F32), shape((16, COLUMNS), F32),
+            ),
+            [pltpu.VMEM((2, 128, 128), F32)],
+            pieces, shares,
         )
     return (result.reshape(volume.shape), grad_input.reshape(volume.shape), first_grad, second_grad)
 

time: 102 us -> 101 us (level)
  no operation moved by 1% of the time
where the time goes in v6:
time: 101 us
  blocking collectives  56.3 us (56%)
  starting transfers between devices  24.7 us (24%)
  waiting for transfers between devices  10.2 us (10%)
  Pallas kernels  7.52 us (7%)
    ppermute x1, starting transfers between devices, body(): far = lax.ppermute(near, 'sy', [(i, (i + SYH) % SY) for i in range(SY)])  16.3 us
    all_to_all x1, blocking collectives, body(): lax.all_to_all(pieces, PENCIL, 0, 0, tiled=True, axis_index_groups=FAR_FO...  12.5 us
    all_to_all x1, blocking collectives, body(): lax.all_to_all(packed, ('sy', 'filt'), 0, 0, tiled=True, axis_index_group...  12.4 us
    all_to_all x1, blocking collectives, body(): lax.all_to_all(shares, ('sy', 'filt'), 0, 0, tiled=True, axis_index_group...  12 us
    all_to_all x1, blocking collectives, body(): lax.all_to_all(pieces, PENCIL, 0, 0, tiled=True, axis_index_groups=SIXTEENS)  10.8 us
    all_to_all x1, blocking collectives, body(): lax.all_to_all(pieces, PENCIL, 0, 0, tiled=True, axis_index_groups=FOURS)  8.67 us
    pallas_call x7, Pallas kernels, call(): pl.pallas_call(kernel, out_shape=out_shape, scratch_shapes=scratch, compi...  6.88 us
    all_to_all x1, waiting for transfers between devices, body(): filters = lax.all_to_all(filters, 'filt', 0, 0, tiled=True)  6.62 us
  transfers between devices with their start and end apart: 4, of which 2 were waited for; matrix products, arithmetic and copies ran while one was open for 1% of the time, Pallas kernels for 1%

profile of v6, /device:TPU:1, one launch (start us, length us, event | category | flops | bytes accessed | tf_op | source)
XLA Modules:
  0.0 101.1 jit_solution(7765644958378887190)
XLA Ops:
  0.6 0.0 copy-start
  0.6 0.0 copy-start.1
  0.7 0.8 pad_maximum_fusion.1.near_ref
  1.5 16.3 %collective-permute-start = (bf16[256,128]{1,0:T(8,128)(2,1)S(1)}, bf16[256,128]{1,0:T(8,128)(2,1)S(1)}, u32[]{:S(2)}, u32[]{:S(2)}) collective-permute-start(bf16[256,128]{1,0:T(8,128)(2,1)S(1)} %pad_maximum_fusion.1.near_ref), channel_id=1, source_target_pairs={{0,256},{64,320},{128,384},{192,448},{256,0},{320,64},{384,128},{4... | collective-permute-start | bytes 196616 | tf_op jit(solution)/shard_map/halves_exchange/ppermute | solution.py:325
  17.7 0.0 copy-done
  17.8 0.8 broadcast_in_dim.3
  18.6 4.0 %all-to-all-start = ((bf16[4,2,16,1728]{3,2,1,0:T(8,128)(2,1)}), bf16[4,2,16,1728]{3,2,1,0:T(8,128)(2,1)S(1)}, u32[]{:S(2)}, u32[]{:S(2)}) async-start(bf16[4,2,16,1728]{3,2,1,0:T(8,128)(2,1)} %broadcast_in_dim.3), calls=%async_computation | async-start | bytes 917504 | tf_op jit(solution)/shard_map/filters_exchange/all_to_all | solution.py:336
  22.6 0.0 collective-permute-done.far_ref
  22.6 0.6 pack_windows.1
  23.2 6.6 %all-to-all-done.filters_ref = bf16[4,2,16,1728]{3,2,1,0:T(8,128)(2,1)S(1)} async-done(((bf16[4,2,16,1728]{3,2,1,0:T(8,128)(2,1)}), bf16[4,2,16,1728]{3,2,1,0:T(8,128)(2,1)S(1)}, u32[]{:S(2)}, u32[]{:S(2)}) %all-to-all-start) | async-done | bytes 442400 | tf_op jit(solution)/shard_map/filters_exchange/all_to_all | solution.py:336
  29.9 12.4 %all_to_all.30.in_ref = bf16[16,64,128]{2,1,0:T(8,128)(2,1)S(1)} all-to-all(bf16[16,64,128]{2,1,0:T(8,128)(2,1)S(1)} %pack_windows.1), channel_id=1, replica_groups={{0,1,2,3,64,65,66,67,128,129,130,131,192,193,194,195},{256,257,258,259,..., dimensions={0} | all-to-all | bytes 524288 | tf_op jit(solution)/shard_map/windows_exchange/all_to_all | solution.py:339
  42.2 0.2 unpack_windows.1.own_ref
  42.5 3.8 %collective-permute-start.2 = (bf16[1024,128]{1,0:T(8,128)(2,1)S(1)}, bf16[1024,128]{1,0:T(8,128)(2,1)S(1)}, u32[]{:S(2)}, u32[]{:S(2)}) collective-permute-start(bf16[1024,128]{1,0:T(8,128)(2,1)S(1)} %unpack_windows.1.own_ref), channel_id=1, source_target_pairs={{0,316},{4,0},{8,4},{12,8},{16,12},{20,16},{24,20},{28,24},{32,28}... | collective-permute-start | bytes 786440 | tf_op jit(solution)/shard_map/z_rim_exchange/ppermute | solution.py:344
  46.2 0.6 collective-permute-start.1
  46.9 0.8 prepare.1
  47.7 3.5 %collective-permute-done.2.above_ref = bf16[1024,128]{1,0:T(8,128)(2,1)S(1)} collective-permute-done((bf16[1024,128]{1,0:T(8,128)(2,1)S(1)}, bf16[1024,128]{1,0:T(8,128)(2,1)S(1)}, u32[]{:S(2)}, u32[]{:S(2)}) %collective-permute-start.2) | collective-permute-done | bytes 262176 | tf_op jit(solution)/shard_map/z_rim_exchange/ppermute | solution.py:344
  51.2 0.0 collective-permute-done.1.below_ref
  51.2 4.8 %layers.1 = bf16[4,64,1024]{2,1,0:T(8,128)(2,1)S(1)} custom-call(bf16[1024,128]{1,0:T(8,128)(2,1)S(1)} %collective-permute-done.1.below_ref, bf16[1024,128]{1,0:T(8,128)(2,1)S(1)} %unpack_windows.1.own_ref, bf16[1024,128]{1,0:T(8,128)(2,1)S(1)} %collective-permute-done.2.above_ref, bf16[2,256,768]{2,1,0:T(8,128)(2,1)S(1)} %get-tuple-element.15.weights, ...), custom_call_target="tpu_custom_call" | custom-call | tf_op jit(solution)/shard_map/layers/pallas_call | solution.py:70
  56.0 12.0 %all_to_all.31.in_ref.refs_1_ = bf16[16,16,1024]{2,1,0:T(8,128)(2,1)S(1)} all-to-all(bf16[16,16,1024]{2,1,0:T(8,128)(2,1)S(1)} %bitcast.7), channel_id=1, replica_groups={{0,1,2,3,64,65,66,67,128,129,130,131,192,193,194,195},{256,257,258,259,..., dimensions={0} | all-to-all | bytes 1048576 | tf_op jit(solution)/shard_map/blocks_exchange/all_to_all | solution.py:371
  68.0 0.1 split_shares.1
  68.1 8.7 %all_to_all.32.in_ref = bf16[4,16,256]{2,1,0:T(8,128)(2,1)S(1)} all-to-all(bf16[4,16,256]{2,1,0:T(8,128)(2,1)S(1)} %split_shares.1), channel_id=1, replica_groups={{0,4,8,12},{16,20,24,28},{32,36,40,44},{48,52,56,60},{64,68,72,76},{80,..., dimensions={0} | all-to-all | bytes 65536 | tf_op jit(solution)/shard_map/near_sum_exchange/all_to_all | solution.py:375
  76.8 12.5 %all_to_all.33.in_ref = bf16[4,16,256]{2,1,0:T(8,128)(2,1)S(1)} all-to-all(bf16[4,16,256]{2,1,0:T(8,128)(2,1)S(1)} %near_sum_exchange.1), channel_id=1, replica_groups={{0,16,32,48},{4,20,36,52},{8,24,40,56},{12,28,44,60},{64,80,96,112},{68..., dimensions={0} | all-to-all | bytes 65536 | tf_op jit(solution)/shard_map/far_sum_exchange/all_to_all | solution.py:378
  89.2 10.8 %all_to_all.34.refs_0_ = bf16[16,16,256]{2,1,0:T(8,128)(2,1)S(1)} all-to-all(bf16[16,16,256]{2,1,0:T(8,128)(2,1)S(1)} %far_sum_exchange.1), channel_id=1, replica_groups={{0,4,8,12,64,68,72,76,128,132,136,140,192,196,200,204},{16,20,24,28,80,..., dimensions={0} | all-to-all | bytes 262144 | tf_op jit(solution)/shard_map/spread_exchange/all_to_all | solution.py:381
  100.1 1.0 finish.1
  (4 shorter events, 0.0 us)
Async XLA Ops:
  0.6 17.1 %copy-start = (bf16[16,1728]{1,0:T(8,128)(2,1)S(1)}, bf16[16,1728]{1,0:T(8,128)(2,1)}, u32[]{:S(2)}) copy-start(bf16[16,1728]{1,0:T(8,128)(2,1)} %param.6) | copy-start | bytes 165892
  0.6 17.1 %copy-start.1 = (bf16[16,1728]{1,0:T(8,128)(2,1)S(1)}, bf16[16,1728]{1,0:T(8,128)(2,1)}, u32[]{:S(2)}) copy-start(bf16[16,1728]{1,0:T(8,128)(2,1)} %param.5) | copy-start | bytes 165892
  1.5 21.1 %collective-permute-start = (bf16[256,128]{1,0:T(8,128)(2,1)S(1)}, bf16[256,128]{1,0:T(8,128)(2,1)S(1)}, u32[]{:S(2)}, u32[]{:S(2)}) collective-permute-start(bf16[256,128]{1,0:T(8,128)(2,1)S(1)} %pad_maximum_fusion.1.near_ref), channel_id=1, source_target_pairs={{0,256},{64,320},{128,384},{192,448},{256,0},{320,64},{384,128},{4... | collective-permute-start | bytes 196616 | tf_op jit(solution)/shard_map/halves_exchange/ppermute | solution.py:325
  18.6 11.3 %all-to-all-start = ((bf16[4,2,16,1728]{3,2,1,0:T(8,128)(2,1)}), bf16[4,2,16,1728]{3,2,1,0:T(8,128)(2,1)S(1)}, u32[]{:S(2)}, u32[]{:S(2)}) async-start(bf16[4,2,16,1728]{3,2,1,0:T(8,128)(2,1)} %broadcast_in_dim.3), calls=%async_computation | async-start | bytes 917504 | tf_op jit(solution)/shard_map/filters_exchange/all_to_all | solution.py:336
  42.5 8.7 %collective-permute-start.2 = (bf16[1024,128]{1,0:T(8,128)(2,1)S(1)}, bf16[1024,128]{1,0:T(8,128)(2,1)S(1)}, u32[]{:S(2)}, u32[]{:S(2)}) collective-permute-start(bf16[1024,128]{1,0:T(8,128)(2,1)S(1)} %unpack_windows.1.own_ref), channel_id=1, source_target_pairs={{0,316},{4,0},{8,4},{12,8},{16,12},{20,16},{24,20},{28,24},{32,28}... | collective-permute-start | bytes 786440 | tf_op jit(solution)/shard_map/z_rim_exchange/ppermute | solution.py:344
  46.2 5.0 %collective-permute-start.1 = (bf16[1024,128]{1,0:T(8,128)(2,1)S(1)}, bf16[1024,128]{1,0:T(8,128)(2,1)S(1)}, u32[]{:S(2)}, u32[]{:S(2)}) collective-permute-start(bf16[1024,128]{1,0:T(8,128)(2,1)S(1)} %unpack_windows.1.own_ref), channel_id=1, source_target_pairs={{0,4},{4,8},{8,12},{12,16},{16,20},{20,24},{24,28},{28,32},{32,36}... | collective-permute-start | bytes 786440 | tf_op jit(solution)/shard_map/z_rim_exchange/ppermute | solution.py:343

commit v7 on v6

--- a/solution.py
+++ b/solution.py
@@ -169,14 +169,6 @@
                     )
 
 
-def prepare_kernel(own_ref, filters_ref, weights, weights_t, field):
-    for layer in range(2):
-        fill_forward(weights.at[layer], filters_ref, layer)
-        fill_backward(weights_t.at[layer], filters_ref, layer)
-    for z in range(ZB):
-        store_field(field, z, own_ref, z)
-
-
 def convolved(planes, weights, transposed):
     rows = planes[0].shape[0]
     planes = jnp.concatenate(planes, axis=1)
@@ -196,8 +188,20 @@
     )
 
 
+def prepare_kernel(own_ref, filters_ref, weights, weights_t, field, pre_own, act_own):
+    for layer in range(2):
+        fill_forward(weights.at[layer], filters_ref, layer)
+        fill_backward(weights_t.at[layer], filters_ref, layer)
+    for z in range(ZB):
+        store_field(field, z, own_ref, z)
+    for at in range(2):
+        pre = convolved([field[at + b] for b in range(3)], weights[0], True)
+        pre_own[at] = pre
+        store_taps(act_own, at, softplus(pre).astype(BF).astype(F32))
+
+
 def main_kernel(
-    below_ref, own_ref, above_ref, weights, weights_t, field_own, out_ref,
+    below_ref, own_ref, above_ref, weights, weights_t, field_own, pre_own, act_own, out_ref,
     field, act, delta_2, delta_1, pre_1, cells_0, cells_1, cells_2, cells_3,
 ):
     half = lax.axis_index("sy") // SYH
@@ -218,12 +222,15 @@
     for z in range(ZB):
         store_field(field, z, below_ref, z)
         store_field(field, ZB + z, above_ref, z)
-    for z in range(10):
+    def act_rows(z, rows):
+        return act_own[z - 4, rows, :] if z in (4, 5) else act[z, rows, :]
+
+    for z in (0, 1, 2, 3, 6, 7, 8, 9):
         pre = convolved([field_rows(z + b, slice(0, PLANE)) for b in range(3)], weights[0], True)
         pre_1[z] = pre
         store_taps(act, z, softplus(pre).astype(BF).astype(F32))
     for z in range(8):
-        pre = convolved(planes(act, z), weights[1], True)
+        pre = convolved([act_rows(z + b, slice(None)) for b in range(3)], weights[1], True)
         cotangent = slab_rows(z + 2, 2 * Y, (XW - 4) * Y)
         low = lanes_of(cotangent.shape) < C
         cotangent = jnp.where(low, turned(cotangent, C), cotangent)
@@ -234,7 +241,8 @@
             cells_2[z - 2] = delta[2 * Y : (2 + XB) * Y]
     for z in range(6):
         back = convolved(planes(delta_2, z), weights_t[1], False)
-        delta = (back * sigmoid(pre_1[z + 2, 2 * Y : (XW - 4) * Y, :])).astype(BF).astype(F32)
+        pre = pre_own[z - 2] if z in (2, 3) else pre_1[z + 2]
+        delta = (back * sigmoid(pre[2 * Y : (XW - 4) * Y])).astype(BF).astype(F32)
         store_taps(delta_1, z, delta)
         if 1 <= z < 5:
             cells_3[z - 1] = delta[Y : (1 + XB) * Y]
@@ -254,9 +262,6 @@
         for to in range(SYH):
             first = QUARTER + at * 64
             out_ref[to, :, first : first + 64] = flat[:, to * 64 : to * 64 + 64]
-    def act_rows(z, rows):
-        return act[z, rows, :]
-
     for base, cells, source, at in ((0, cells_3, field_rows, 3), (HALF, cells_2, act_rows, 2)):
         flat = jnp.transpose(cells[...].reshape(count, 128))[0:C, :].astype(BF)
         for b in range(3):
@@ -343,9 +348,12 @@
         below = lax.ppermute(own, PENCIL, along_z(1))
         above = lax.ppermute(own, PENCIL, along_z(-1))
     with jax.named_scope("prepare"):
-        weights, weights_t, field_own = call(
+        prepared = call(
             prepare_kernel,
-            (shape((2, 256, 768), BF), shape((2, 768, 256), BF), shape((ZB, PLANE, 256), BF)),
+            (
+                shape((2, 256, 768), BF), shape((2, 768, 256), BF), shape((ZB, PLANE, 256), BF),
+                shape((2, (XW - 2) * Y, 128), F32), shape((2, (XW - 2) * Y, 256), BF),
+            ),
             [],
             own, filters,
         )
@@ -364,7 +372,7 @@
                 pltpu.VMEM((ZB, XB * Y, 128), F32),
                 pltpu.VMEM((ZB, XB * Y, 128), F32),
             ],
-            below, own, above, weights, weights_t, field_own,
+            below, own, above, *prepared,
         )
     with jax.named_scope("blocks_exchange"):
         shares = partial.reshape(BLOCKS, 16, QUARTER + 128)

time: 101 us -> 101 us (level)
  transfers between devices with their start and end apart: 4 -> 4, of which waited for: 2 -> 2; matrix products, arithmetic and copies ran while one was open for 1% -> 1% of each run, Pallas kernels for 1% -> 2%
where the time goes in v7:
time: 101 us
  blocking collectives  56.3 us (56%)
  starting transfers between devices  24.7 us (24%)
  waiting for transfers between devices  9.89 us (10%)
  Pallas kernels  7.49 us (7%)
    ppermute x1, starting transfers between devices, body(): far = lax.ppermute(near, 'sy', [(i, (i + SYH) % SY) for i in range(SY)])  16.3 us
    all_to_all x1, blocking collectives, body(): lax.all_to_all(pieces, PENCIL, 0, 0, tiled=True, axis_index_groups=FAR_FO...  12.5 us
    all_to_all x1, blocking collectives, body(): lax.all_to_all(packed, ('sy', 'filt'), 0, 0, tiled=True, axis_index_group...  12.4 us
    all_to_all x1, blocking collectives, body(): lax.all_to_all(shares, ('sy', 'filt'), 0, 0, tiled=True, axis_index_group...  11.9 us
    all_to_all x1, blocking collectives, body(): lax.all_to_all(pieces, PENCIL, 0, 0, tiled=True, axis_index_groups=SIXTEENS)  10.8 us
    all_to_all x1, blocking collectives, body(): lax.all_to_all(pieces, PENCIL, 0, 0, tiled=True, axis_index_groups=FOURS)  8.69 us
    pallas_call x7, Pallas kernels, call(): pl.pallas_call(kernel, out_shape=out_shape, scratch_shapes=scratch, compi...  6.85 us
    all_to_all x1, waiting for transfers between devices, body(): filters = lax.all_to_all(filters, 'filt', 0, 0, tiled=True)  6.62 us
  transfers between devices with their start and end apart: 4, of which 2 were waited for; matrix products, arithmetic and copies ran while one was open for 1% of the time, Pallas kernels for 2%

profile of v7, /device:TPU:1, one launch (start us, length us, event | category | flops | bytes accessed | tf_op | source)
XLA Modules:
  0.0 100.8 jit_solution(18231153351932393048)
XLA Ops:
  0.6 0.0 copy-start
  0.6 0.0 copy-start.1
  0.7 0.8 pad_maximum_fusion.1.near_ref
  1.5 16.3 %collective-permute-start = (bf16[256,128]{1,0:T(8,128)(2,1)S(1)}, bf16[256,128]{1,0:T(8,128)(2,1)S(1)}, u32[]{:S(2)}, u32[]{:S(2)}) collective-permute-start(bf16[256,128]{1,0:T(8,128)(2,1)S(1)} %pad_maximum_fusion.1.near_ref), channel_id=1, source_target_pairs={{0,256},{64,320},{128,384},{192,448},{256,0},{320,64},{384,128},{4... | collective-permute-start | bytes 196616 | tf_op jit(solution)/shard_map/halves_exchange/ppermute | solution.py:330
  17.7 0.0 copy-done
  17.8 0.8 broadcast_in_dim.3
  18.6 4.0 %all-to-all-start = ((bf16[4,2,16,1728]{3,2,1,0:T(8,128)(2,1)}), bf16[4,2,16,1728]{3,2,1,0:T(8,128)(2,1)S(1)}, u32[]{:S(2)}, u32[]{:S(2)}) async-start(bf16[4,2,16,1728]{3,2,1,0:T(8,128)(2,1)} %broadcast_in_dim.3), calls=%async_computation | async-start | bytes 917504 | tf_op jit(solution)/shard_map/filters_exchange/all_to_all | solution.py:341
  22.6 0.0 collective-permute-done.far_ref
  22.6 0.6 pack_windows.1
  23.2 6.6 %all-to-all-done.filters_ref = bf16[4,2,16,1728]{3,2,1,0:T(8,128)(2,1)S(1)} async-done(((bf16[4,2,16,1728]{3,2,1,0:T(8,128)(2,1)}), bf16[4,2,16,1728]{3,2,1,0:T(8,128)(2,1)S(1)}, u32[]{:S(2)}, u32[]{:S(2)}) %all-to-all-start) | async-done | bytes 442400 | tf_op jit(solution)/shard_map/filters_exchange/all_to_all | solution.py:341
  29.9 12.4 %all_to_all.30.in_ref = bf16[16,64,128]{2,1,0:T(8,128)(2,1)S(1)} all-to-all(bf16[16,64,128]{2,1,0:T(8,128)(2,1)S(1)} %pack_windows.1), channel_id=1, replica_groups={{0,1,2,3,64,65,66,67,128,129,130,131,192,193,194,195},{256,257,258,259,..., dimensions={0} | all-to-all | bytes 524288 | tf_op jit(solution)/shard_map/windows_exchange/all_to_all | solution.py:344
  42.2 0.2 unpack_windows.1.own_ref
  42.5 3.8 %collective-permute-start.2 = (bf16[1024,128]{1,0:T(8,128)(2,1)S(1)}, bf16[1024,128]{1,0:T(8,128)(2,1)S(1)}, u32[]{:S(2)}, u32[]{:S(2)}) collective-permute-start(bf16[1024,128]{1,0:T(8,128)(2,1)S(1)} %unpack_windows.1.own_ref), channel_id=1, source_target_pairs={{0,316},{4,0},{8,4},{12,8},{16,12},{20,16},{24,20},{28,24},{32,28}... | collective-permute-start | bytes 786440 | tf_op jit(solution)/shard_map/z_rim_exchange/ppermute | solution.py:349
  46.2 0.6 collective-permute-start.1
  46.9 1.1 %prepare.1 = (bf16[2,256,768]{2,1,0:T(8,128)(2,1)S(1)}, bf16[2,768,256]{2,1,0:T(8,128)(2,1)S(1)}, bf16[4,256,256]{2,1,0:T(8,128)(2,1)S(1)}, f32[2,224,128]{2,1,0:T(8,128)S(1)}, bf16[2,224,256]{2,1,0:T(8,128)(2,1)S(1)}) custom-call(bf16[1024,128]{1,0:T(8,128)(2,1)S(1)} %unpack_windows.1.own_ref, bf16[4,2,16,1728]{3,2,1,0:T(8,128)(2,1)S(1)} %all-to-all-done.filters_ref), custom_call_target="tpu_custom_call" | custom-call | tf_op jit(solution)/shard_map/prepare/pallas_call | solution.py:70
  47.9 3.3 %collective-permute-done.2.above_ref = bf16[1024,128]{1,0:T(8,128)(2,1)S(1)} collective-permute-done((bf16[1024,128]{1,0:T(8,128)(2,1)S(1)}, bf16[1024,128]{1,0:T(8,128)(2,1)S(1)}, u32[]{:S(2)}, u32[]{:S(2)}) %collective-permute-start.2) | collective-permute-done | bytes 262176 | tf_op jit(solution)/shard_map/z_rim_exchange/ppermute | solution.py:349
  51.2 0.0 collective-permute-done.1.below_ref
  51.2 4.5 %layers.1 = bf16[4,64,1024]{2,1,0:T(8,128)(2,1)S(1)} custom-call(bf16[1024,128]{1,0:T(8,128)(2,1)S(1)} %collective-permute-done.1.below_ref, bf16[1024,128]{1,0:T(8,128)(2,1)S(1)} %unpack_windows.1.own_ref, bf16[1024,128]{1,0:T(8,128)(2,1)S(1)} %collective-permute-done.2.above_ref, bf16[2,256,768]{2,1,0:T(8,128)(2,1)S(1)} %get-tuple-element.17.weights, ...), custom_call_target="tpu_custom_call" | custom-call | tf_op jit(solution)/shard_map/layers/pallas_call | solution.py:70
  55.7 11.9 %all_to_all.31.in_ref.refs_1_ = bf16[16,16,1024]{2,1,0:T(8,128)(2,1)S(1)} all-to-all(bf16[16,16,1024]{2,1,0:T(8,128)(2,1)S(1)} %bitcast.7), channel_id=1, replica_groups={{0,1,2,3,64,65,66,67,128,129,130,131,192,193,194,195},{256,257,258,259,..., dimensions={0} | all-to-all | bytes 1048576 | tf_op jit(solution)/shard_map/blocks_exchange/all_to_all | solution.py:379
  67.6 0.1 split_shares.1
  67.7 8.7 %all_to_all.32.in_ref = bf16[4,16,256]{2,1,0:T(8,128)(2,1)S(1)} all-to-all(bf16[4,16,256]{2,1,0:T(8,128)(2,1)S(1)} %split_shares.1), channel_id=1, replica_groups={{0,4,8,12},{16,20,24,28},{32,36,40,44},{48,52,56,60},{64,68,72,76},{80,..., dimensions={0} | all-to-all | bytes 65536 | tf_op jit(solution)/shard_map/near_sum_exchange/all_to_all | solution.py:383
  76.4 12.5 %all_to_all.33.in_ref = bf16[4,16,256]{2,1,0:T(8,128)(2,1)S(1)} all-to-all(bf16[4,16,256]{2,1,0:T(8,128)(2,1)S(1)} %near_sum_exchange.1), channel_id=1, replica_groups={{0,16,32,48},{4,20,36,52},{8,24,40,56},{12,28,44,60},{64,80,96,112},{68..., dimensions={0} | all-to-all | bytes 65536 | tf_op jit(solution)/shard_map/far_sum_exchange/all_to_all | solution.py:386
  88.9 10.8 %all_to_all.34.refs_0_ = bf16[16,16,256]{2,1,0:T(8,128)(2,1)S(1)} all-to-all(bf16[16,16,256]{2,1,0:T(8,128)(2,1)S(1)} %far_sum_exchange.1), channel_id=1, replica_groups={{0,4,8,12,64,68,72,76,128,132,136,140,192,196,200,204},{16,20,24,28,80,..., dimensions={0} | all-to-all | bytes 262144 | tf_op jit(solution)/shard_map/spread_exchange/all_to_all | solution.py:389
  99.8 1.0 finish.1
  (4 shorter events, 0.0 us)
Async XLA Ops:
  0.6 17.1 %copy-start = (bf16[16,1728]{1,0:T(8,128)(2,1)S(1)}, bf16[16,1728]{1,0:T(8,128)(2,1)}, u32[]{:S(2)}) copy-start(bf16[16,1728]{1,0:T(8,128)(2,1)} %param.6) | copy-start | bytes 165892
  0.6 17.1 %copy-start.1 = (bf16[16,1728]{1,0:T(8,128)(2,1)S(1)}, bf16[16,1728]{1,0:T(8,128)(2,1)}, u32[]{:S(2)}) copy-start(bf16[16,1728]{1,0:T(8,128)(2,1)} %param.5) | copy-start | bytes 165892
  1.5 21.1 %collective-permute-start = (bf16[256,128]{1,0:T(8,128)(2,1)S(1)}, bf16[256,128]{1,0:T(8,128)(2,1)S(1)}, u32[]{:S(2)}, u32[]{:S(2)}) collective-permute-start(bf16[256,128]{1,0:T(8,128)(2,1)S(1)} %pad_maximum_fusion.1.near_ref), channel_id=1, source_target_pairs={{0,256},{64,320},{128,384},{192,448},{256,0},{320,64},{384,128},{4... | collective-permute-start | bytes 196616 | tf_op jit(solution)/shard_map/halves_exchange/ppermute | solution.py:330
  18.6 11.3 %all-to-all-start = ((bf16[4,2,16,1728]{3,2,1,0:T(8,128)(2,1)}), bf16[4,2,16,1728]{3,2,1,0:T(8,128)(2,1)S(1)}, u32[]{:S(2)}, u32[]{:S(2)}) async-start(bf16[4,2,16,1728]{3,2,1,0:T(8,128)(2,1)} %broadcast_in_dim.3), calls=%async_computation | async-start | bytes 917504 | tf_op jit(solution)/shard_map/filters_exchange/all_to_all | solution.py:341
  42.5 8.7 %collective-permute-start.2 = (bf16[1024,128]{1,0:T(8,128)(2,1)S(1)}, bf16[1024,128]{1,0:T(8,128)(2,1)S(1)}, u32[]{:S(2)}, u32[]{:S(2)}) collective-permute-start(bf16[1024,128]{1,0:T(8,128)(2,1)S(1)} %unpack_windows.1.own_ref), channel_id=1, source_target_pairs={{0,316},{4,0},{8,4},{12,8},{16,12},{20,16},{24,20},{28,24},{32,28}... | collective-permute-start | bytes 786440 | tf_op jit(solution)/shard_map/z_rim_exchange/ppermute | solution.py:349
  46.2 5.0 %collective-permute-start.1 = (bf16[1024,128]{1,0:T(8,128)(2,1)S(1)}, bf16[1024,128]{1,0:T(8,128)(2,1)S(1)}, u32[]{:S(2)}, u32[]{:S(2)}) collective-permute-start(bf16[1024,128]{1,0:T(8,128)(2,1)S(1)} %unpack_windows.1.own_ref), channel_id=1, source_target_pairs={{0,4},{4,8},{8,12},{12,16},{16,20},{20,24},{24,28},{28,32},{32,36}... | collective-permute-start | bytes 786440 | tf_op jit(solution)/shard_map/z_rim_exchange/ppermute | solution.py:348

commit v8 on v7

--- a/solution.py
+++ b/solution.py
@@ -227,7 +227,8 @@
 
     for z in (0, 1, 2, 3, 6, 7, 8, 9):
         pre = convolved([field_rows(z + b, slice(0, PLANE)) for b in range(3)], weights[0], True)
-        pre_1[z] = pre
+        if 2 <= z < 8:
+            pre_1[z] = pre
         store_taps(act, z, softplus(pre).astype(BF).astype(F32))
     for z in range(8):
         pre = convolved([act_rows(z + b, slice(None)) for b in range(3)], weights[1], True)

time: 101 us -> 101 us (level)
  no operation moved by 1% of the time
where the time goes in v8:
time: 101 us
  blocking collectives  56.3 us (56%)
  starting transfers between devices  24.7 us (24%)
  waiting for transfers between devices  9.89 us (10%)
  Pallas kernels  7.49 us (7%)
    ppermute x1, starting transfers between devices, body(): far = lax.ppermute(near, 'sy', [(i, (i + SYH) % SY) for i in range(SY)])  16.3 us
    all_to_all x1, blocking collectives, body(): lax.all_to_all(pieces, PENCIL, 0, 0, tiled=True, axis_index_groups=FAR_FO...  12.5 us
    all_to_all x1, blocking collectives, body(): lax.all_to_all(packed, ('sy', 'filt'), 0, 0, tiled=True, axis_index_group...  12.4 us
    all_to_all x1, blocking collectives, body(): lax.all_to_all(shares, ('sy', 'filt'), 0, 0, tiled=True, axis_index_group...  11.9 us
    all_to_all x1, blocking collectives, body(): lax.all_to_all(pieces, PENCIL, 0, 0, tiled=True, axis_index_groups=SIXTEENS)  10.8 us
    all_to_all x1, blocking collectives, body(): lax.all_to_all(pieces, PENCIL, 0, 0, tiled=True, axis_index_groups=FOURS)  8.69 us
    pallas_call x7, Pallas kernels, call(): pl.pallas_call(kernel, out_shape=out_shape, scratch_shapes=scratch, compi...  6.85 us
    all_to_all x1, waiting for transfers between devices, body(): filters = lax.all_to_all(filters, 'filt', 0, 0, tiled=True)  6.62 us
  transfers between devices with their start and end apart: 4, of which 2 were waited for; matrix products, arithmetic and copies ran while one was open for 1% of the time, Pallas kernels for 2%

profile of v8, /device:TPU:1, one launch (start us, length us, event | category | flops | bytes accessed | tf_op | source)
XLA Modules:
  0.0 100.8 jit_solution(18231153351932393048)
XLA Ops:
  0.6 0.0 copy-start
  0.6 0.0 copy-start.1
  0.7 0.8 pad_maximum_fusion.1.near_ref
  1.5 16.3 %collective-permute-start = (bf16[256,128]{1,0:T(8,128)(2,1)S(1)}, bf16[256,128]{1,0:T(8,128)(2,1)S(1)}, u32[]{:S(2)}, u32[]{:S(2)}) collective-permute-start(bf16[256,128]{1,0:T(8,128)(2,1)S(1)} %pad_maximum_fusion.1.near_ref), channel_id=1, source_target_pairs={{0,256},{64,320},{128,384},{192,448},{256,0},{320,64},{384,128},{4... | collective-permute-start | bytes 196616 | tf_op jit(solution)/shard_map/halves_exchange/ppermute | solution.py:331
  17.7 0.0 copy-done
  17.8 0.8 broadcast_in_dim.3
  18.6 4.0 %all-to-all-start = ((bf16[4,2,16,1728]{3,2,1,0:T(8,128)(2,1)}), bf16[4,2,16,1728]{3,2,1,0:T(8,128)(2,1)S(1)}, u32[]{:S(2)}, u32[]{:S(2)}) async-start(bf16[4,2,16,1728]{3,2,1,0:T(8,128)(2,1)} %broadcast_in_dim.3), calls=%async_computation | async-start | bytes 917504 | tf_op jit(solution)/shard_map/filters_exchange/all_to_all | solution.py:342
  22.6 0.0 collective-permute-done.far_ref
  22.6 0.6 pack_windows.1
  23.2 6.6 %all-to-all-done.filters_ref = bf16[4,2,16,1728]{3,2,1,0:T(8,128)(2,1)S(1)} async-done(((bf16[4,2,16,1728]{3,2,1,0:T(8,128)(2,1)}), bf16[4,2,16,1728]{3,2,1,0:T(8,128)(2,1)S(1)}, u32[]{:S(2)}, u32[]{:S(2)}) %all-to-all-start) | async-done | bytes 442400 | tf_op jit(solution)/shard_map/filters_exchange/all_to_all | solution.py:342
  29.9 12.4 %all_to_all.30.in_ref = bf16[16,64,128]{2,1,0:T(8,128)(2,1)S(1)} all-to-all(bf16[16,64,128]{2,1,0:T(8,128)(2,1)S(1)} %pack_windows.1), channel_id=1, replica_groups={{0,1,2,3,64,65,66,67,128,129,130,131,192,193,194,195},{256,257,258,259,..., dimensions={0} | all-to-all | bytes 524288 | tf_op jit(solution)/shard_map/windows_exchange/all_to_all | solution.py:345
  42.2 0.2 unpack_windows.1.own_ref
  42.5 3.8 %collective-permute-start.2 = (bf16[1024,128]{1,0:T(8,128)(2,1)S(1)}, bf16[1024,128]{1,0:T(8,128)(2,1)S(1)}, u32[]{:S(2)}, u32[]{:S(2)}) collective-permute-start(bf16[1024,128]{1,0:T(8,128)(2,1)S(1)} %unpack_windows.1.own_ref), channel_id=1, source_target_pairs={{0,316},{4,0},{8,4},{12,8},{16,12},{20,16},{24,20},{28,24},{32,28}... | collective-permute-start | bytes 786440 | tf_op jit(solution)/shard_map/z_rim_exchange/ppermute | solution.py:350
  46.2 0.6 collective-permute-start.1
  46.9 1.1 %prepare.1 = (bf16[2,256,768]{2,1,0:T(8,128)(2,1)S(1)}, bf16[2,768,256]{2,1,0:T(8,128)(2,1)S(1)}, bf16[4,256,256]{2,1,0:T(8,128)(2,1)S(1)}, f32[2,224,128]{2,1,0:T(8,128)S(1)}, bf16[2,224,256]{2,1,0:T(8,128)(2,1)S(1)}) custom-call(bf16[1024,128]{1,0:T(8,128)(2,1)S(1)} %unpack_windows.1.own_ref, bf16[4,2,16,1728]{3,2,1,0:T(8,128)(2,1)S(1)} %all-to-all-done.filters_ref), custom_call_target="tpu_custom_call" | custom-call | tf_op jit(solution)/shard_map/prepare/pallas_call | solution.py:70
  47.9 3.3 %collective-permute-done.2.above_ref = bf16[1024,128]{1,0:T(8,128)(2,1)S(1)} collective-permute-done((bf16[1024,128]{1,0:T(8,128)(2,1)S(1)}, bf16[1024,128]{1,0:T(8,128)(2,1)S(1)}, u32[]{:S(2)}, u32[]{:S(2)}) %collective-permute-start.2) | collective-permute-done | bytes 262176 | tf_op jit(solution)/shard_map/z_rim_exchange/ppermute | solution.py:350
  51.2 0.0 collective-permute-done.1.below_ref
  51.2 4.5 %layers.1 = bf16[4,64,1024]{2,1,0:T(8,128)(2,1)S(1)} custom-call(bf16[1024,128]{1,0:T(8,128)(2,1)S(1)} %collective-permute-done.1.below_ref, bf16[1024,128]{1,0:T(8,128)(2,1)S(1)} %unpack_windows.1.own_ref, bf16[1024,128]{1,0:T(8,128)(2,1)S(1)} %collective-permute-done.2.above_ref, bf16[2,256,768]{2,1,0:T(8,128)(2,1)S(1)} %get-tuple-element.17.weights, ...), custom_call_target="tpu_custom_call" | custom-call | tf_op jit(solution)/shard_map/layers/pallas_call | solution.py:70
  55.7 11.9 %all_to_all.31.in_ref.refs_1_ = bf16[16,16,1024]{2,1,0:T(8,128)(2,1)S(1)} all-to-all(bf16[16,16,1024]{2,1,0:T(8,128)(2,1)S(1)} %bitcast.7), channel_id=1, replica_groups={{0,1,2,3,64,65,66,67,128,129,130,131,192,193,194,195},{256,257,258,259,..., dimensions={0} | all-to-all | bytes 1048576 | tf_op jit(solution)/shard_map/blocks_exchange/all_to_all | solution.py:380
  67.6 0.1 split_shares.1
  67.7 8.7 %all_to_all.32.in_ref = bf16[4,16,256]{2,1,0:T(8,128)(2,1)S(1)} all-to-all(bf16[4,16,256]{2,1,0:T(8,128)(2,1)S(1)} %split_shares.1), channel_id=1, replica_groups={{0,4,8,12},{16,20,24,28},{32,36,40,44},{48,52,56,60},{64,68,72,76},{80,..., dimensions={0} | all-to-all | bytes 65536 | tf_op jit(solution)/shard_map/near_sum_exchange/all_to_all | solution.py:384
  76.4 12.5 %all_to_all.33.in_ref = bf16[4,16,256]{2,1,0:T(8,128)(2,1)S(1)} all-to-all(bf16[4,16,256]{2,1,0:T(8,128)(2,1)S(1)} %near_sum_exchange.1), channel_id=1, replica_groups={{0,16,32,48},{4,20,36,52},{8,24,40,56},{12,28,44,60},{64,80,96,112},{68..., dimensions={0} | all-to-all | bytes 65536 | tf_op jit(solution)/shard_map/far_sum_exchange/all_to_all | solution.py:387
  88.9 10.8 %all_to_all.34.refs_0_ = bf16[16,16,256]{2,1,0:T(8,128)(2,1)S(1)} all-to-all(bf16[16,16,256]{2,1,0:T(8,128)(2,1)S(1)} %far_sum_exchange.1), channel_id=1, replica_groups={{0,4,8,12,64,68,72,76,128,132,136,140,192,196,200,204},{16,20,24,28,80,..., dimensions={0} | all-to-all | bytes 262144 | tf_op jit(solution)/shard_map/spread_exchange/all_to_all | solution.py:390
  99.8 1.0 finish.1
  (4 shorter events, 0.0 us)
Async XLA Ops:
  0.6 17.1 %copy-start = (bf16[16,1728]{1,0:T(8,128)(2,1)S(1)}, bf16[16,1728]{1,0:T(8,128)(2,1)}, u32[]{:S(2)}) copy-start(bf16[16,1728]{1,0:T(8,128)(2,1)} %param.6) | copy-start | bytes 165892
  0.6 17.1 %copy-start.1 = (bf16[16,1728]{1,0:T(8,128)(2,1)S(1)}, bf16[16,1728]{1,0:T(8,128)(2,1)}, u32[]{:S(2)}) copy-start(bf16[16,1728]{1,0:T(8,128)(2,1)} %param.5) | copy-start | bytes 165892
  1.5 21.1 %collective-permute-start = (bf16[256,128]{1,0:T(8,128)(2,1)S(1)}, bf16[256,128]{1,0:T(8,128)(2,1)S(1)}, u32[]{:S(2)}, u32[]{:S(2)}) collective-permute-start(bf16[256,128]{1,0:T(8,128)(2,1)S(1)} %pad_maximum_fusion.1.near_ref), channel_id=1, source_target_pairs={{0,256},{64,320},{128,384},{192,448},{256,0},{320,64},{384,128},{4... | collective-permute-start | bytes 196616 | tf_op jit(solution)/shard_map/halves_exchange/ppermute | solution.py:331
  18.6 11.3 %all-to-all-start = ((bf16[4,2,16,1728]{3,2,1,0:T(8,128)(2,1)}), bf16[4,2,16,1728]{3,2,1,0:T(8,128)(2,1)S(1)}, u32[]{:S(2)}, u32[]{:S(2)}) async-start(bf16[4,2,16,1728]{3,2,1,0:T(8,128)(2,1)} %broadcast_in_dim.3), calls=%async_computation | async-start | bytes 917504 | tf_op jit(solution)/shard_map/filters_exchange/all_to_all | solution.py:342
  42.5 8.7 %collective-permute-start.2 = (bf16[1024,128]{1,0:T(8,128)(2,1)S(1)}, bf16[1024,128]{1,0:T(8,128)(2,1)S(1)}, u32[]{:S(2)}, u32[]{:S(2)}) collective-permute-start(bf16[1024,128]{1,0:T(8,128)(2,1)S(1)} %unpack_windows.1.own_ref), channel_id=1, source_target_pairs={{0,316},{4,0},{8,4},{12,8},{16,12},{20,16},{24,20},{28,24},{32,28}... | collective-permute-start | bytes 786440 | tf_op jit(solution)/shard_map/z_rim_exchange/ppermute | solution.py:350
  46.2 5.0 %collective-permute-start.1 = (bf16[1024,128]{1,0:T(8,128)(2,1)S(1)}, bf16[1024,128]{1,0:T(8,128)(2,1)S(1)}, u32[]{:S(2)}, u32[]{:S(2)}) collective-permute-start(bf16[1024,128]{1,0:T(8,128)(2,1)S(1)} %unpack_windows.1.own_ref), channel_id=1, source_target_pairs={{0,4},{4,8},{8,12},{12,16},{16,20},{20,24},{24,28},{28,32},{32,36}... | collective-permute-start | bytes 786440 | tf_op jit(solution)/shard_map/z_rim_exchange/ppermute | solution.py:349
